TPU v7x, 256 devices: a whole 4x4x8 slice. The times are simulated.
256 devices in a mesh: dp: 64 (over y, z, core), width: 4 (over x).
Axes of the slice: x: 4, y: 4, z: 8, core: 2. Of those that a mesh axis runs over, the one named last changes fastest.
Arguments:
- queries: bfloat16 [8192, 3584], P('dp', 'width'), may hold values from -8 to 8
- codes: bfloat16 [8192, 3584], P('dp', 'width'), may hold values from -8 to 8
- pairing: int32 [64, 128], P('dp'), may hold values from 0 to 127, each once within a row
- neg_blocks: int32 [64, 4], replicated, may hold values from 0 to 63, as said below
- neg_count: int32 [64], replicated, may hold values from 1 to 4
Outputs:
- grad_queries: float32 [8192, 3584], P('dp', 'width')
- grad_codes: float32 [8192, 3584], P('dp', 'width')
Inputs may be any that keep to these rules, and one draw needn't show every extreme that they name: Row b of pairing orders 0 to 127, each once. `neg_blocks`: row b names 4 different blocks, none of them b.
All inputs are finite; a program needn't handle non-finite values.
Results may differ from a plain program's by a relative error of at most 0.0023.
Values may be sent and summed in bfloat16 or wider, within the bound.
No kernel may reach another device: no remote copies, remote signals or barrier semaphores. Data moves between devices by JAX's collectives and lax.ppermute only.
A program may use at most 64 MiB of HBM per device.

v0:
```python
import functools

import jax
import jax.numpy as jnp
from jax import lax
from jax.experimental import pallas as pl
from jax.experimental.pallas import tpu as pltpu
from jax.sharding import Mesh, PartitionSpec as P

INV_TEMP = 50.0
NY, NZ, NC, NX = 4, 8, 2, 4
BLK = 128
SLOTS = 4
QUARTER = BLK // NX
HALF = BLK // 2
CAP_SMALL = 18
CAP_FULL = 80
LOWEST = -3.0e38
DP = ("y", "z", "c")
LIST_LEN = 88
GRANT_PER_SLOT = 5 * 2**14
F32 = jnp.float32
BF16 = jnp.bfloat16
VMEM = pltpu.VMEM
SMEM = pltpu.SMEM


def wrap(v, n):
    return v & (n - 1)


def grant(own, cap):
    return pltpu.CompilerParams(vmem_limit_bytes=own + GRANT_PER_SLOT * cap)


def spec_v():
    return pl.BlockSpec(memory_space=VMEM)


def spec_s():
    return pl.BlockSpec(memory_space=SMEM)


def list_kernel(neg_ref, count_ref, neg_v, count_v, ent_ref, over_ref):
    y, z, c, x = (lax.axis_index(name) for name in ("y", "z", "c", "x"))

    def push(k, e, j, take):
        ent_ref[0, k] = e
        ent_ref[1, k] = j
        return k + take.astype(jnp.int32)

    def first(e, k):
        b = ((y << 3) + wrap(z + e, NZ)) * NC + c
        count = count_ref[b]
        for r in range(SLOTS):
            n = neg_ref[r, b]
            take = (r < count) & (wrap(n >> 1, NZ) == z)
            k = push(k, e, 2 * wrap((n >> 4) - y, NY) + ((n & 1) ^ c), take)
        return k

    def second(j, k):
        b = ((wrap(y + (j >> 1), NY) << 3) + z) * NC + ((j & 1) ^ c)
        count = count_ref[b]
        for r in range(SLOTS):
            n = neg_ref[r, b]
            take = (r < count) & ((n >> 4) == y) & ((n & 1) == c)
            k = push(k, wrap((n >> 1) - z, NZ), j, take)
        return k

    n1 = lax.fori_loop(0, NZ, first, push(0, 0, 0, jnp.bool_(True)))
    n2 = lax.fori_loop(0, NY * NC, second, push(n1, 0, 0, jnp.bool_(True)))
    for i, v in enumerate((n1, n2, x, y, z, c)):
        ent_ref[2, i] = v
    blocks = count_v.shape[1]
    shape = (NZ, blocks)
    group = lax.broadcasted_iota(jnp.int32, shape, 0)
    b = lax.broadcasted_iota(jnp.int32, shape, 1)
    count = jnp.broadcast_to(count_v[...], shape)

    def rows_of(n):
        return ((n >> 4) << 1) + (n & 1)

    def cols_of(n):
        return wrap(n >> 1, NZ)

    def ones(mask):
        return jnp.where(mask, 1.0, 0.0)

    to_cols, to_rows = jnp.zeros(shape, F32), jnp.zeros(shape, F32)
    for r in range(SLOTS):
        n = jnp.broadcast_to(neg_v[pl.ds(r, 1), :], shape)
        to_cols += ones((cols_of(n) == group) & (r < count))
        to_rows += ones((rows_of(n) == group) & (r < count))
    tiles = dot_nt(ones(rows_of(b) == group), to_cols) + dot_nt(to_rows, ones(cols_of(b) == group))
    over_ref[0] = (jnp.max(tiles) + 2.0 > CAP_SMALL).astype(jnp.int32)


def build_list(neg_blocks, neg_count):
    neg = neg_blocks.T
    return pl.pallas_call(
        list_kernel,
        out_shape=[
            jax.ShapeDtypeStruct((3, LIST_LEN), jnp.int32),
            jax.ShapeDtypeStruct((1,), jnp.int32),
        ],
        in_specs=[spec_s(), spec_s(), spec_v(), spec_v()],
        out_specs=[spec_s(), spec_s()],
        compiler_params=grant(2 * 2**20, 0),
        name="block_list",
    )(neg, neg_count, neg, neg_count.reshape(1, -1))


NQ, NCODE = 9, 8


def fill_queries(q_refs, qs):
    own, l1, l2, l3, r1, r2, r3, r4, l4 = q_refs
    for e, ref in ((0, own), (1, l1), (2, l2), (3, l3), (7, r1), (6, r2), (5, r3)):
        qs[e] = ref[...]
    qs[4, :HALF] = r4[...]
    qs[4, HALF:] = l4[...]


def dot_nt(a, b):
    return lax.dot_general(a, b, (((1,), (1,)), ((), ())), preferred_element_type=F32)


def dot_nn(a, b):
    return lax.dot_general(a, b, (((1,), (0,)), ((), ())), preferred_element_type=F32)


def dot_tn(a, b):
    return lax.dot_general(a, b, (((0,), (0,)), ((), ())), preferred_element_type=F32)


def quarter_starts(x):
    return [pl.multiple_of(wrap(x + d, NX) * QUARTER, QUARTER) for d in range(NX)]


def score_kernel(ent, *refs):
    q_refs, c_refs = refs[:NQ], refs[NQ : NQ + NCODE]
    outs = refs[NQ + NCODE : NQ + NCODE + NX]
    qs, cs, tile = refs[NQ + NCODE + NX :]
    fill_queries(q_refs, qs)
    for j, ref in enumerate(c_refs):
        cs[j] = ref[...]
    n1, n2 = ent[2, 0], ent[2, 1]
    starts = quarter_starts(ent[2, 2])

    def emit(k, s):
        tile[...] = s
        for out, start in zip(outs, starts):
            out[k] = tile[pl.ds(start, QUARTER), :]

    def first(k, _):
        emit(k, dot_nt(qs[ent[0, k]], cs[ent[1, k]]))
        return 0

    def second(k, _):
        emit(k, dot_nt(cs[ent[1, k]], qs[ent[0, k]]))
        return 0

    lax.fori_loop(0, n1, first, 0)
    lax.fori_loop(n1, n2, second, 0)


def partial_scores(cap, ent, q_parts, c_parts):
    feats = q_parts[0].shape[-1]
    return pl.pallas_call(
        score_kernel,
        out_shape=[jax.ShapeDtypeStruct((cap, QUARTER, BLK), F32)] * NX,
        in_specs=[spec_s()] + [spec_v()] * (NQ + NCODE),
        out_specs=[spec_v()] * NX,
        scratch_shapes=[
            VMEM((NZ, BLK, feats), BF16),
            VMEM((NY * NC, BLK, feats), BF16),
            VMEM((BLK, BLK), F32),
        ],
        compiler_params=grant(8 * 2**20, cap),
        name="scores",
    )(ent, *q_parts, *c_parts)


def group_lane(ent, k, n1):
    y, z, c = ent[2, 3], ent[2, 4], ent[2, 5]
    e, j = ent[0, k], ent[1, k]
    first = wrap(z + e, NZ)
    second = NZ + 2 * wrap(y + (j >> 1), NY) + ((j & 1) ^ c)
    return jnp.where(k < n1, first, second)


def lanes_of(rows):
    return lax.broadcasted_iota(jnp.int32, (rows, BLK), 1)


def stats_kernel(ent, s0, s1, s2, s3, s_ref, st_ref, top, tot):
    n1, n2 = ent[2, 0], ent[2, 1]
    top[...] = jnp.full(top.shape, LOWEST, F32)
    tot[...] = jnp.zeros(tot.shape, F32)

    def first(k, _):
        s = INV_TEMP * ((s0[k] + s2[k]) + (s1[k] + s3[k]))
        s_ref[k] = s
        g = group_lane(ent, k, n1)
        top[g] = jnp.maximum(top[g], s)
        return 0

    lax.fori_loop(0, n2, first, 0)
    for g in range(2 * NZ):
        top[g] = jnp.broadcast_to(jnp.max(top[g], axis=1, keepdims=True), (QUARTER, BLK))

    def second(k, _):
        g = group_lane(ent, k, n1)
        tot[g] = tot[g] + jnp.exp(s_ref[k] - top[g])
        return 0

    lax.fori_loop(0, n2, second, 0)
    lane = lanes_of(QUARTER)
    m = jnp.full((QUARTER, BLK), LOWEST, F32)
    l = jnp.zeros((QUARTER, BLK), F32)
    for g in range(2 * NZ):
        m = jnp.where(lane == g, top[g], m)
        l = jnp.where(lane == g, jnp.sum(tot[g], axis=1, keepdims=True), l)
    st_ref[0] = m
    st_ref[1] = l


def local_stats(cap, ent, parts):
    return pl.pallas_call(
        stats_kernel,
        out_shape=[
            jax.ShapeDtypeStruct((cap, QUARTER, BLK), F32),
            jax.ShapeDtypeStruct((2, QUARTER, BLK), F32),
        ],
        in_specs=[spec_s()] + [spec_v()] * NX,
        out_specs=[spec_v()] * 2,
        scratch_shapes=[VMEM((2 * NZ, QUARTER, BLK), F32)] * 2,
        compiler_params=grant(2 * 2**20, cap),
        name="local_stats",
    )(ent, *parts)


def coef_kernel(ent, s_ref, prow, za, zb, ya, yb, g_ref, top, inv, hits):
    n1, n2 = ent[2, 0], ent[2, 1]
    lane = lanes_of(QUARTER)
    over_z, over_yc = merge(za[...], zb[...]), merge(ya[...], yb[...])
    m, l = (jnp.where(lane < NZ, a, b) for a, b in zip(over_z, over_yc))
    for g in range(2 * NZ):
        here, shape = lane == g, (QUARTER, BLK)
        top[g] = jnp.broadcast_to(jnp.max(jnp.where(here, m, LOWEST), axis=1, keepdims=True), shape)
        inv[g] = jnp.broadcast_to(1.0 / jnp.sum(jnp.where(here, l, 0.0), axis=1, keepdims=True), shape)
    start = pl.multiple_of(ent[2, 2] * QUARTER, QUARTER)
    hit = (prow[...] == lax.broadcasted_iota(jnp.int32, (BLK, BLK), 0)).astype(F32)
    hits[0] = hit.T
    hits[1] = hit

    def probs(k):
        g = group_lane(ent, k, n1)
        return jnp.exp(s_ref[k] - top[g]) * inv[g]

    def far(k, _):
        g_ref[k] = (0.5 * probs(k)).astype(BF16)
        return 0

    lax.fori_loop(1, n1, far, 0)
    lax.fori_loop(n1 + 1, n2, far, 0)
    g_ref[0] = (0.5 * (probs(0) - hits[0, pl.ds(start, QUARTER), :])).astype(BF16)
    g_ref[n1] = (0.5 * (probs(n1) - hits[1, pl.ds(start, QUARTER), :])).astype(BF16)


def coefficients(cap, ent, scores, pairing, *stats):
    return pl.pallas_call(
        coef_kernel,
        out_shape=jax.ShapeDtypeStruct((cap, QUARTER, BLK), BF16),
        in_specs=[spec_s()] + [spec_v()] * 6,
        out_specs=spec_v(),
        scratch_shapes=[
            VMEM((2 * NZ, QUARTER, BLK), F32),
            VMEM((2 * NZ, QUARTER, BLK), F32),
            VMEM((2, BLK, BLK), F32),
        ],
        compiler_params=grant(2 * 2**20, cap),
        name="coefficients",
    )(ent, scores, pairing, *stats)


def query_grad_kernel(ent, *refs):
    quarters, c_refs, refs = refs[:NX], refs[NX : NX + NCODE], refs[NX + NCODE :]
    g_ref, own, p1, p2, p3, p4a, p4b, m1, m2, m3 = refs[:10]
    cs, acc = refs[10:]
    n1, n2 = ent[2, 0], ent[2, 1]
    for j, ref in enumerate(c_refs):
        cs[j] = ref[...]
    acc[...] = jnp.zeros(acc.shape, F32)
    starts = quarter_starts(ent[2, 2])

    def coefs(k):
        for ref, start in zip(quarters, starts):
            g_ref[k, pl.ds(start, QUARTER), :] = ref[k]
        return g_ref[k]

    def first(k, _):
        acc[ent[0, k]] += dot_nn(coefs(k), cs[ent[1, k]])
        return 0

    def second(k, _):
        acc[ent[0, k]] += dot_tn(coefs(k), cs[ent[1, k]])
        return 0

    lax.fori_loop(0, n1, first, 0)
    lax.fori_loop(n1, n2, second, 0)
    own[...] = INV_TEMP * acc[0]
    for e, out in ((1, p1), (2, p2), (3, p3), (7, m1), (6, m2), (5, m3)):
        out[...] = (INV_TEMP * acc[e]).astype(BF16)
    p4a[...] = (INV_TEMP * acc[4, :HALF]).astype(BF16)
    p4b[...] = (INV_TEMP * acc[4, HALF:]).astype(BF16)


def query_grads(cap, ent, coefs, c_parts):
    feats = c_parts[0].shape[-1]
    part = jax.ShapeDtypeStruct((BLK, feats), BF16)
    half = jax.ShapeDtypeStruct((HALF, feats), BF16)
    return pl.pallas_call(
        query_grad_kernel,
        out_shape=[
            jax.ShapeDtypeStruct((cap, BLK, BLK), BF16),
            jax.ShapeDtypeStruct((BLK, feats), F32),
            *[part, part, part, half, half, part, part, part],
        ],
        in_specs=[spec_s()] + [spec_v()] * (NX + NCODE),
        out_specs=[spec_v()] * 10,
        scratch_shapes=[
            VMEM((NY * NC, BLK, feats), BF16),
            VMEM((NZ, BLK, feats), F32),
        ],
        compiler_params=grant(10 * 2**20, cap),
        cost_estimate=pl.CostEstimate(flops=10**9, bytes_accessed=12 * 10**6, transcendentals=0),
        name="query_grads",
    )(ent, *coefs, *c_parts)


def code_grad_kernel(ent, g_ref, *refs):
    q_refs, (own, pc1, pc2, pc3, po, qs, acc) = refs[:NQ], refs[NQ:]
    n1, n2 = ent[2, 0], ent[2, 1]
    fill_queries(q_refs, qs)
    acc[...] = jnp.zeros(acc.shape, F32)

    def first(k, _):
        acc[ent[1, k]] += dot_tn(g_ref[k], qs[ent[0, k]])
        return 0

    def second(k, _):
        acc[ent[1, k]] += dot_nn(g_ref[k], qs[ent[0, k]])
        return 0

    lax.fori_loop(0, n1, first, 0)
    lax.fori_loop(n1, n2, second, 0)
    own[...] = INV_TEMP * acc[0]
    for d, out in ((1, pc1), (2, pc2), (3, pc3)):
        out[...] = (INV_TEMP * acc[2 * d]).astype(BF16)
    for d in range(NY):
        po[d] = (INV_TEMP * acc[2 * d + 1]).astype(BF16)


def code_grads(ent, coefs, q_parts):
    feats = q_parts[0].shape[-1]
    part = jax.ShapeDtypeStruct((BLK, feats), BF16)
    return pl.pallas_call(
        code_grad_kernel,
        out_shape=[
            jax.ShapeDtypeStruct((BLK, feats), F32),
            *[part, part, part],
            jax.ShapeDtypeStruct((NY, BLK, feats), BF16),
        ],
        in_specs=[spec_s()] + [spec_v()] * (1 + NQ),
        out_specs=[spec_v()] * 5,
        scratch_shapes=[VMEM((NZ, BLK, feats), BF16), VMEM((NY * NC, BLK, feats), F32)],
        compiler_params=grant(10 * 2**20, coefs.shape[0]),
        cost_estimate=pl.CostEstimate(flops=10**9, bytes_accessed=12 * 10**6, transcendentals=0),
        name="code_grads",
    )(ent, coefs, *q_parts)


def shift(value, axis, by):
    n = {"x": NX, "y": NY, "z": NZ, "c": NC}[axis]
    return lax.ppermute(value, axis, [(i, (i + by) % n) for i in range(n)])


def merge(a, b):
    m = jnp.maximum(a[0], b[0])
    return m, a[1] * jnp.exp(a[0] - m) + b[1] * jnp.exp(b[0] - m)


def small_kernel(fn, name, out_shape, *args):
    def kernel(*refs):
        outs = fn(*(ref[...] for ref in refs[: len(args)]))
        for ref, out in zip(refs[len(args) :], outs):
            ref[...] = out

    return pl.pallas_call(
        kernel,
        out_shape=out_shape,
        in_specs=[spec_v()] * len(args),
        out_specs=[spec_v()] * len(out_shape),
        compiler_params=grant(4 * 2**20, 0),
        name=name,
    )(*args)


def merge_both(za, zb, ya, yb):
    return jnp.stack(merge(za, zb)), jnp.stack(merge(ya, yb))


def swap(value, axis, bit):
    n = {"y": NY, "z": NZ, "c": NC}[axis]
    return lax.ppermute(value, axis, [(i, i ^ bit) for i in range(n)])


def exchange(st):
    like = [jax.ShapeDtypeStruct(st.shape, F32)] * 2
    over_z, over_yc = st, st
    for z_bit, (axis, bit) in ((1, ("c", 1)), (2, ("y", 1))):
        over_z, over_yc = small_kernel(
            merge_both, "merge", like, over_z, swap(over_z, "z", z_bit), over_yc, swap(over_yc, axis, bit)
        )
    return over_z, swap(over_z, "z", 4), over_yc, swap(over_yc, "y", 2)


def from_others(value, axis):
    return shift(value, axis, -1), shift(value, axis, 2), shift(value, axis, 1)


def gather(queries, codes, ent):
    r1, l1 = shift(queries, "z", 1), shift(queries, "z", -1)
    c_mine = (codes, *from_others(codes, "y"))
    c_parts = tuple(v for part in c_mine for v in (part, shift(part, "c", 1)))
    r1, l1, ent = lax.optimization_barrier((r1, l1, ent))
    r2, l2 = shift(r1, "z", 1), shift(l1, "z", -1)
    r3, l3 = shift(r2, "z", 1), shift(l2, "z", -1)
    r4, l4 = shift(r3[:HALF], "z", 1), shift(l3[HALF:], "z", -1)
    return (queries, l1, l2, l3, r1, r2, r3, r4, l4), c_parts, ent


def total(*parts):
    out = parts[0].astype(F32)
    for p in parts[1:]:
        out = out + p.astype(F32)
    return out


def join_halves(b, d, r, l):
    r = jnp.concatenate([total(b, r[:HALF]).astype(BF16), r[HALF:]], axis=0)
    return r, jnp.concatenate([l[:HALF], total(d, l[HALF:]).astype(BF16)], axis=0)


def join(a, b, r, l):
    return total(a, r).astype(BF16), total(b, l).astype(BF16)


def join_codes(other, *parts):
    return [total(part, other[d + 1]).astype(BF16) for d, part in enumerate(parts)]


def reduce_queries(g, p1, p2, p3, p4a, p4b, m1, m2, m3):
    like = [jax.ShapeDtypeStruct(p1.shape, BF16)] * 2
    r, l = shift(p4a, "z", 1), shift(p4b, "z", -1)
    r, l = small_kernel(join_halves, "join_halves", like, r, l, p3, m3)
    for a, b in ((p2, m2), (p1, m1)):
        r, l = shift(r, "z", 1), shift(l, "z", -1)
        r, l = small_kernel(join, "join", like, r, l, a, b)
    return (shift(r, "z", 1), shift(l, "z", -1)), g


def reduce_codes(po, *parts):
    like = [jax.ShapeDtypeStruct(parts[0].shape, BF16)] * 3
    other = shift(po, "c", 1)
    parts = small_kernel(join_codes, "join_codes", like, other, *parts)
    return other[0], *(shift(part, "y", d + 1) for d, part in enumerate(parts))


def run(cap, queries, codes, pairing, neg_blocks, neg_count):
    ent, over = build_list(neg_blocks, neg_count)
    with jax.named_scope("gather"):
        q_parts, c_parts, ent = gather(queries, codes, ent)
    o0, o1, o2, o3 = partial_scores(cap, ent, q_parts, c_parts)
    with jax.named_scope("scores_over_x"):
        parts = (o0, shift(o1, "x", 1), shift(o2, "x", 2), shift(o3, "x", -1))
    scores, st = local_stats(cap, ent, parts)
    with jax.named_scope("stats"):
        stats = exchange(st)
    coefs = coefficients(cap, ent, scores, pairing, *stats)
    with jax.named_scope("coefs_over_x"):
        coefs = (coefs, *from_others(coefs, "x"))
    g, own_q, *parts = query_grads(cap, ent, coefs, c_parts)
    with jax.named_scope("reduce"):
        from_z, g = reduce_queries(g, *parts)
        own_c, pc1, pc2, pc3, po = code_grads(ent, g, q_parts)
        from_yc = reduce_codes(po, pc1, pc2, pc3)
    return over, (total(own_q, *from_z), total(own_c, *from_yc))


def long_query_grad_kernel(ent, *refs):
    s_refs, st_refs, prow = refs[:NX], refs[NX : 2 * NX], refs[2 * NX]
    c_refs, refs = refs[2 * NX + 1 : 2 * NX + 1 + NCODE], refs[2 * NX + 1 + NCODE :]
    g_ref, own, p1, p2, p3, p4a, p4b, m1, m2, m3 = refs[:10]
    cs, acc, st, tile = refs[10:]
    n1, n2 = ent[2, 0], ent[2, 1]
    for j, ref in enumerate(c_refs):
        cs[j] = ref[...]
    acc[...] = jnp.zeros(acc.shape, F32)
    starts = quarter_starts(ent[2, 2])
    for ref, start in zip(st_refs, starts):
        st[:, pl.ds(start, QUARTER), :] = ref[...]
    lane = lanes_of(BLK)

    def coefs(k, hit):
        here = lane == group_lane(ent, k, n1)
        m = jnp.max(jnp.where(here, st[0], LOWEST), axis=1, keepdims=True)
        l = jnp.sum(jnp.where(here, st[1], 0.0), axis=1, keepdims=True)
        for ref, start in zip(s_refs, starts):
            tile[pl.ds(start, QUARTER), :] = ref[k]
        g = (0.5 * (jnp.exp(tile[...] - m) * (1.0 / l) - hit)).astype(BF16)
        g_ref[k] = g
        return g

    def first(k, hit):
        acc[ent[0, k]] += dot_nn(coefs(k, hit), cs[ent[1, k]])

    def second(k, hit):
        acc[ent[0, k]] += dot_tn(coefs(k, hit), cs[ent[1, k]])

    def far(fn, k, _):
        fn(k, 0.0)
        return 0

    hit = (prow[...] == lax.broadcasted_iota(jnp.int32, (BLK, BLK), 0)).astype(F32)
    first(0, hit.T)
    lax.fori_loop(1, n1, functools.partial(far, first), 0)
    second(n1, hit)
    lax.fori_loop(n1 + 1, n2, functools.partial(far, second), 0)
    own[...] = INV_TEMP * acc[0]
    for e, out in ((1, p1), (2, p2), (3, p3), (7, m1), (6, m2), (5, m3)):
        out[...] = (INV_TEMP * acc[e]).astype(BF16)
    p4a[...] = (INV_TEMP * acc[4, :HALF]).astype(BF16)
    p4b[...] = (INV_TEMP * acc[4, HALF:]).astype(BF16)


def long_query_grads(cap, ent, scores, stats, pairing, c_parts):
    feats = c_parts[0].shape[-1]
    part = jax.ShapeDtypeStruct((BLK, feats), BF16)
    half = jax.ShapeDtypeStruct((HALF, feats), BF16)
    return pl.pallas_call(
        long_query_grad_kernel,
        out_shape=[
            jax.ShapeDtypeStruct((cap, BLK, BLK), BF16),
            jax.ShapeDtypeStruct((BLK, feats), F32),
            *[part, part, part, half, half, part, part, part],
        ],
        in_specs=[spec_s()] + [spec_v()] * (2 * NX + 1 + NCODE),
        out_specs=[spec_v()] * 10,
        scratch_shapes=[
            VMEM((NY * NC, BLK, feats), BF16),
            VMEM((NZ, BLK, feats), F32),
            VMEM((2, BLK, BLK), F32),
            VMEM((BLK, BLK), F32),
        ],
        compiler_params=grant(10 * 2**20, cap),
        cost_estimate=pl.CostEstimate(flops=10**9, bytes_accessed=12 * 10**6, transcendentals=10**5),
        name="query_grads",
    )(ent, *scores, *stats, pairing, *c_parts)


def near_stats(st, left, right, other):
    two = merge(left, st)
    return jnp.stack(two), jnp.stack(merge(two, right)), jnp.stack(merge(st, other))


def final_stats(three, pair, z1, z2, y1, y2, y3):
    over_z = merge(merge(three, z1), z2)
    over_yc = merge(merge(pair, y1), merge(y2, y3))
    first = lanes_of(QUARTER) < NZ
    return (jnp.stack([jnp.where(first, a, b) for a, b in zip(over_z, over_yc)]),)


def long_exchange(cap, scores, st):
    others = from_others(scores, "x")
    left, right, other = shift(st, "z", 1), shift(st, "z", -1), shift(st, "c", 1)
    like = jax.ShapeDtypeStruct(st.shape, F32)
    two, three, pair = small_kernel(near_stats, "near_stats", [like] * 3, st, left, right, other)
    z1, z2 = shift(three, "z", 3), shift(two, "z", -3)
    y1, y2, y3 = from_others(pair, "y")
    (st,) = small_kernel(final_stats, "final_stats", [like], three, pair, z1, z2, y1, y2, y3)
    return (scores, *others), (st, *from_others(st, "x"))


def long_run(cap, queries, codes, pairing, neg_blocks, neg_count):
    ent, over = build_list(neg_blocks, neg_count)
    with jax.named_scope("gather"):
        q_parts, c_parts, ent = gather(queries, codes, ent)
    o0, o1, o2, o3 = partial_scores(cap, ent, q_parts, c_parts)
    with jax.named_scope("scores_over_x"):
        parts = (o0, shift(o1, "x", 1), shift(o2, "x", 2), shift(o3, "x", -1))
    scores, st = local_stats(cap, ent, parts)
    with jax.named_scope("stats"):
        scores, stats = long_exchange(cap, scores, st)
    g, own_q, p1, p2, p3, p4a, p4b, m1, m2, m3 = long_query_grads(
        cap, ent, scores, stats, pairing, c_parts
    )
    own_c, pc1, pc2, pc3, po = code_grads(ent, g, q_parts)
    with jax.named_scope("reduce"):
        from_z = reduce_queries(g, p1, p2, p3, p4a, p4b, m1, m2, m3)[0]
        from_yc = reduce_codes(po, pc1, pc2, pc3)
    return over, (total(own_q, *from_z), total(own_c, *from_yc))


def local(*args):
    over, short = run(CAP_SMALL, *args)
    return lax.while_loop(
        lambda state: state[0] > 0,
        lambda state: (jnp.int32(0), long_run(CAP_FULL, *args)[1]),
        (over[0], short),
    )[1]


def solution(mesh):
    grid = Mesh(mesh.devices.reshape(NY, NZ, NC, NX), ("y", "z", "c", "x"))
    in_specs = (P(DP, "x"), P(DP, "x"), P(DP, None), P(), P())
    out_specs = (P(DP, "x"), P(DP, "x"))
    return jax.shard_map(local, mesh=grid, in_specs=in_specs, out_specs=out_specs, check_vma=False)
```

profile of v0, /device:TPU:24, one launch (start us, length us, event | category | flops | bytes accessed | tf_op | source)
XLA Modules:
  0.0 135.4 jit_solution(7736598663459585178)
XLA Ops:
  2.6 4.0 %collective-permute-start.45 = (bf16[128,896]{1,0:T(8,128)(2,1)}, bf16[128,896]{1,0:T(8,128)(2,1)S(1)}, u32[]{:S(2)}, u32[]{:S(2)}) collective-permute-start(bf16[128,896]{1,0:T(8,128)(2,1)} %refs_0_.3), channel_id=1, source_target_pairs={{0,56},{8,0},{16,8},{24,16},{32,24},{40,32},{48,40},{56,48},{1,57}... | collective-permute-start | bytes 688136 | tf_op jit(solution)/shard_map/gather/ppermute | solution.py:386
  8.7 3.6 %collective-permute-done.44.refs_4_ = bf16[128,896]{1,0:T(8,128)(2,1)S(1)} collective-permute-done((bf16[128,896]{1,0:T(8,128)(2,1)}, bf16[128,896]{1,0:T(8,128)(2,1)S(1)}, u32[]{:S(2)}, u32[]{:S(2)}) %collective-permute-start.44) | collective-permute-done | bytes 229408 | tf_op jit(solution)/shard_map/gather/ppermute | solution.py:386
  12.4 3.2 %collective-permute-start.46 = (bf16[128,896]{1,0:T(8,128)(2,1)S(1)}, bf16[128,896]{1,0:T(8,128)(2,1)S(1)}, u32[]{:S(2)}, u32[]{:S(2)}) collective-permute-start(bf16[128,896]{1,0:T(8,128)(2,1)S(1)} %collective-permute-done.45.refs_1_), channel_id=1, source_target_pairs={{0,56},{8,0},{16,8},{24,16},{32,24},{40,32},{48,40},{56,48},{1,57}... | collective-permute-start | bytes 688136 | tf_op jit(solution)/shard_map/gather/ppermute | solution.py:386
  17.3 2.2 %collective-permute-start.57 = (bf16[128,896]{1,0:T(8,128)(2,1)}, bf16[128,896]{1,0:T(8,128)(2,1)S(1)}, u32[]{:S(2)}, u32[]{:S(2)}) collective-permute-start(bf16[128,896]{1,0:T(8,128)(2,1)} %refs_4_.1), channel_id=1, source_target_pairs={{0,64},{64,128},{128,192},{192,0},{1,65},{65,129},{129,193},{193,1... | collective-permute-start | bytes 688136 | tf_op jit(solution)/shard_map/gather/ppermute | solution.py:386
  20.4 3.2 %collective-permute-start.47 = (bf16[128,896]{1,0:T(8,128)(2,1)S(1)}, bf16[128,896]{1,0:T(8,128)(2,1)S(1)}, u32[]{:S(2)}, u32[]{:S(2)}) collective-permute-start(bf16[128,896]{1,0:T(8,128)(2,1)S(1)} %collective-permute-done.46.refs_2_), channel_id=1, source_target_pairs={{0,56},{8,0},{16,8},{24,16},{32,24},{40,32},{48,40},{56,48},{1,57}... | collective-permute-start | bytes 688136 | tf_op jit(solution)/shard_map/gather/ppermute | solution.py:386
  23.6 4.6 %collective-permute-done.53.refs_11_.refs_6_ = bf16[128,896]{1,0:T(8,128)(2,1)S(1)} collective-permute-done((bf16[128,896]{1,0:T(8,128)(2,1)}, bf16[128,896]{1,0:T(8,128)(2,1)S(1)}, u32[]{:S(2)}, u32[]{:S(2)}) %collective-permute-start.53) | collective-permute-done | bytes 229408 | tf_op jit(solution)/shard_map/gather/ppermute | solution.py:386
  30.1 2.5 %collective-permute-start.51 = (bf16[64,896]{1,0:T(8,128)(2,1)S(1)}, bf16[64,896]{1,0:T(8,128)(2,1)S(1)}, u32[]{:S(2)}, u32[]{:S(2)}) collective-permute-start(bf16[64,896]{1,0:T(8,128)(2,1)S(1)} %slice.25), channel_id=1, source_target_pairs={{0,56},{8,0},{16,8},{24,16},{32,24},{40,32},{48,40},{56,48},{1,57}... | collective-permute-start | bytes 344072 | tf_op jit(solution)/shard_map/gather/ppermute | solution.py:386
  32.7 3.0 %collective-permute-done.50.refs_7_ = bf16[64,896]{1,0:T(8,128)(2,1)S(1)} collective-permute-done((bf16[64,896]{1,0:T(8,128)(2,1)S(1)}, bf16[64,896]{1,0:T(8,128)(2,1)S(1)}, u32[]{:S(2)}, u32[]{:S(2)}) %collective-permute-start.50) | collective-permute-done | bytes 114720 | tf_op jit(solution)/shard_map/gather/ppermute | solution.py:386
  35.7 2.8 %scores.3 = (f32[18,32,128]{2,1,0:T(8,128)S(1)}, f32[18,32,128]{2,1,0:T(8,128)S(1)}, f32[18,32,128]{2,1,0:T(8,128)S(1)}, f32[18,32,128]{2,1,0:T(8,128)S(1)}) custom-call(s32[3,88]{1,0:T(4,128)S(1)} %get-tuple-element.120.ent, bf16[128,896]{1,0:T(8,128)(2,1)} %refs_0_.3, bf16[128,896]{1,0:T(8,128)(2,1)S(1)} %collective-permute-done.45.refs_1_, ...), custom_call_target="tpu_custom_call" | custom-call | tf_op jit(solution)/shard_map/scores/pallas_call | solution.py:169
  40.1 2.7 %collective-permute-start.60 = (f32[18,32,128]{2,1,0:T(8,128)S(1)}, f32[18,32,128]{2,1,0:T(8,128)S(1)}, u32[]{:S(2)}, u32[]{:S(2)}) collective-permute-start(f32[18,32,128]{2,1,0:T(8,128)S(1)} %get-tuple-element.125), channel_id=1, source_target_pairs={{0,2},{1,3},{2,0},{3,1},{4,6},{5,7},{6,4},{7,5},{8,10},{9,11},{10,... | collective-permute-start | bytes 884744 | tf_op jit(solution)/shard_map/scores_over_x/ppermute | solution.py:386
  44.3 4.5 %collective-permute-done.59.s1 = f32[18,32,128]{2,1,0:T(8,128)S(1)} collective-permute-done((f32[18,32,128]{2,1,0:T(8,128)S(1)}, f32[18,32,128]{2,1,0:T(8,128)S(1)}, u32[]{:S(2)}, u32[]{:S(2)}) %collective-permute-start.59) | collective-permute-done | bytes 294944 | tf_op jit(solution)/shard_map/scores_over_x/ppermute | solution.py:386
  48.8 6.5 %collective-permute-done.60.s2 = f32[18,32,128]{2,1,0:T(8,128)S(1)} collective-permute-done((f32[18,32,128]{2,1,0:T(8,128)S(1)}, f32[18,32,128]{2,1,0:T(8,128)S(1)}, u32[]{:S(2)}, u32[]{:S(2)}) %collective-permute-start.60) | collective-permute-done | bytes 294944 | tf_op jit(solution)/shard_map/scores_over_x/ppermute | solution.py:386
  56.5 3.8 %collective-permute-done.62.refs_1_ = f32[2,32,128]{2,1,0:T(8,128)S(1)} collective-permute-done((f32[2,32,128]{2,1,0:T(8,128)S(1)}, f32[2,32,128]{2,1,0:T(8,128)S(1)}, u32[]{:S(2)}, u32[]{:S(2)}) %collective-permute-start.62) | collective-permute-done | bytes 32800 | tf_op jit(solution)/shard_map/stats/ppermute | solution.py:416
  60.4 2.5 %collective-permute-start.64 = (f32[2,32,128]{2,1,0:T(8,128)S(1)}, f32[2,32,128]{2,1,0:T(8,128)S(1)}, u32[]{:S(2)}, u32[]{:S(2)}) collective-permute-start(f32[2,32,128]{2,1,0:T(8,128)S(1)} %get-tuple-element.129.refs_0_), channel_id=1, source_target_pairs={{0,16},{8,24},{16,0},{24,8},{32,48},{40,56},{48,32},{56,40},{1,17}... | collective-permute-start | bytes 98312 | tf_op jit(solution)/shard_map/stats/ppermute | solution.py:416
  66.8 2.3 %collective-permute-start.66 = (f32[2,32,128]{2,1,0:T(8,128)S(1)}, f32[2,32,128]{2,1,0:T(8,128)S(1)}, u32[]{:S(2)}, u32[]{:S(2)}) collective-permute-start(f32[2,32,128]{2,1,0:T(8,128)S(1)} %get-tuple-element.131.za), channel_id=1, source_target_pairs={{0,32},{8,40},{16,48},{24,56},{32,0},{40,8},{48,16},{56,24},{1,33}... | collective-permute-start | bytes 98312 | tf_op jit(solution)/shard_map/stats/ppermute | solution.py:416
  69.1 2.2 %collective-permute-start.67 = (f32[2,32,128]{2,1,0:T(8,128)S(1)}, f32[2,32,128]{2,1,0:T(8,128)S(1)}, u32[]{:S(2)}, u32[]{:S(2)}) collective-permute-start(f32[2,32,128]{2,1,0:T(8,128)S(1)} %get-tuple-element.132.ya), channel_id=1, source_target_pairs={{0,128},{64,192},{128,0},{192,64},{1,129},{65,193},{129,1},{193,65... | collective-permute-start | bytes 98312 | tf_op jit(solution)/shard_map/stats/ppermute | solution.py:416
  71.3 3.5 %collective-permute-done.66.zb = f32[2,32,128]{2,1,0:T(8,128)S(1)} collective-permute-done((f32[2,32,128]{2,1,0:T(8,128)S(1)}, f32[2,32,128]{2,1,0:T(8,128)S(1)}, u32[]{:S(2)}, u32[]{:S(2)}) %collective-permute-start.66) | collective-permute-done | bytes 32800 | tf_op jit(solution)/shard_map/stats/ppermute | solution.py:416
  75.7 2.5 %collective-permute-start.68 = (bf16[18,32,128]{2,1,0:T(8,128)(2,1)S(1)}, bf16[18,32,128]{2,1,0:T(8,128)(2,1)S(1)}, u32[]{:S(2)}, u32[]{:S(2)}) collective-permute-start(bf16[18,32,128]{2,1,0:T(8,128)(2,1)S(1)} %coefficients.1.refs_0_), channel_id=1, source_target_pairs={{0,3},{1,0},{2,1},{3,2},{4,7},{5,4},{6,5},{7,6},{8,11},{9,8},{10,9... | collective-permute-start | bytes 442376 | tf_op jit(solution)/shard_map/coefs_over_x/ppermute | solution.py:386
  79.8 2.6 %collective-permute-done.68.refs_1_ = bf16[18,32,128]{2,1,0:T(8,128)(2,1)S(1)} collective-permute-done((bf16[18,32,128]{2,1,0:T(8,128)(2,1)S(1)}, bf16[18,32,128]{2,1,0:T(8,128)(2,1)S(1)}, u32[]{:S(2)}, u32[]{:S(2)}) %collective-permute-start.68) | collective-permute-done | bytes 147488 | tf_op jit(solution)/shard_map/coefs_over_x/ppermute | solution.py:386
  82.5 2.4 %collective-permute-done.69.refs_2_ = bf16[18,32,128]{2,1,0:T(8,128)(2,1)S(1)} collective-permute-done((bf16[18,32,128]{2,1,0:T(8,128)(2,1)S(1)}, bf16[18,32,128]{2,1,0:T(8,128)(2,1)S(1)}, u32[]{:S(2)}, u32[]{:S(2)}) %collective-permute-start.69) | collective-permute-done | bytes 147488 | tf_op jit(solution)/shard_map/coefs_over_x/ppermute | solution.py:386
  86.4 3.0 %query_grads.3 = (bf16[18,128,128]{2,1,0:T(8,128)(2,1)S(1)}, f32[128,896]{1,0:T(8,128)S(1)}, bf16[128,896]{1,0:T(8,128)(2,1)S(1)}, bf16[128,896]{1,0:T(8,128)(2,...) custom-call(s32[3,88]{1,0:T(4,128)S(1)} %get-tuple-element.120.ent, ...), custom_call_target="tpu_custom_call" | custom-call | flops 1000000000 | bytes 12000000 | tf_op jit(solution)/shard_map/query_grads/pallas_call | solution.py:323
  89.5 2.9 %code_grads.3 = (f32[128,896]{1,0:T(8,128)S(1)}, bf16[128,896]{1,0:T(8,128)(2,1)S(1)}, bf16[128,896]{1,0:T(8,128)(2,1)S(1)}, bf16[128,896]{1,0:T(8,128)(2,1)S(1)}, bf16[4,128,896]{2,1,0:T(8,128)(2,1)S(1)}) custom-call(s32[3,88]{1,0:T(4,128)S(1)} %get-tuple-element.120.ent, bf16[18,128,128]{2,1,0:T(8,128)(2,1)S(1)} %get-tuple-element.148.g_ref, ...), custom_call_target="tpu_custom_call" | custom-call | flops 1000000000 | bytes 12000000 | tf_op jit(solution)/shard_map/reduce/code_grads/pallas_call | solution.py:368
  92.6 3.2 %collective-permute-start.72 = (bf16[64,896]{1,0:T(8,128)(2,1)S(1)}, bf16[64,896]{1,0:T(8,128)(2,1)S(1)}, u32[]{:S(2)}, u32[]{:S(2)}) collective-permute-start(bf16[64,896]{1,0:T(8,128)(2,1)S(1)} %get-tuple-element.135), channel_id=1, source_target_pairs={{0,56},{8,0},{16,8},{24,16},{32,24},{40,32},{48,40},{56,48},{1,57}... | collective-permute-start | bytes 344072 | tf_op jit(solution)/shard_map/reduce/ppermute | solution.py:386
  95.8 3.6 %collective-permute-done.71.refs_0_ = bf16[64,896]{1,0:T(8,128)(2,1)S(1)} collective-permute-done((bf16[64,896]{1,0:T(8,128)(2,1)S(1)}, bf16[64,896]{1,0:T(8,128)(2,1)S(1)}, u32[]{:S(2)}, u32[]{:S(2)}) %collective-permute-start.71) | collective-permute-done | bytes 114720 | tf_op jit(solution)/shard_map/reduce/ppermute | solution.py:386
  99.7 3.4 %collective-permute-start.74 = (bf16[128,896]{1,0:T(8,128)(2,1)S(1)}, bf16[128,896]{1,0:T(8,128)(2,1)S(1)}, u32[]{:S(2)}, u32[]{:S(2)}) collective-permute-start(bf16[128,896]{1,0:T(8,128)(2,1)S(1)} %get-tuple-element.139), channel_id=1, source_target_pairs={{0,56},{8,0},{16,8},{24,16},{32,24},{40,32},{48,40},{56,48},{1,57}... | collective-permute-start | bytes 688136 | tf_op jit(solution)/shard_map/reduce/ppermute | solution.py:386
  103.1 5.0 %collective-permute-done.73.refs_0_ = bf16[128,896]{1,0:T(8,128)(2,1)S(1)} collective-permute-done((bf16[128,896]{1,0:T(8,128)(2,1)S(1)}, bf16[128,896]{1,0:T(8,128)(2,1)S(1)}, u32[]{:S(2)}, u32[]{:S(2)}) %collective-permute-start.73) | collective-permute-done | bytes 229408 | tf_op jit(solution)/shard_map/reduce/ppermute | solution.py:386
  109.5 2.1 %collective-permute-start.76 = (bf16[128,896]{1,0:T(8,128)(2,1)S(1)}, bf16[128,896]{1,0:T(8,128)(2,1)S(1)}, u32[]{:S(2)}, u32[]{:S(2)}) collective-permute-start(bf16[128,896]{1,0:T(8,128)(2,1)S(1)} %get-tuple-element.143), channel_id=1, source_target_pairs={{0,56},{8,0},{16,8},{24,16},{32,24},{40,32},{48,40},{56,48},{1,57}... | collective-permute-start | bytes 688136 | tf_op jit(solution)/shard_map/reduce/ppermute | solution.py:386
  111.6 4.4 %collective-permute-done.75.refs_0_ = bf16[128,896]{1,0:T(8,128)(2,1)S(1)} collective-permute-done((bf16[128,896]{1,0:T(8,128)(2,1)S(1)}, bf16[128,896]{1,0:T(8,128)(2,1)S(1)}, u32[]{:S(2)}, u32[]{:S(2)}) %collective-permute-start.75) | collective-permute-done | bytes 229408 | tf_op jit(solution)/shard_map/reduce/ppermute | solution.py:386
  116.1 2.2 %collective-permute-start.77 = (bf16[128,896]{1,0:T(8,128)(2,1)S(1)}, bf16[128,896]{1,0:T(8,128)(2,1)S(1)}, u32[]{:S(2)}, u32[]{:S(2)}) collective-permute-start(bf16[128,896]{1,0:T(8,128)(2,1)S(1)} %get-tuple-element.146), channel_id=1, source_target_pairs={{0,8},{8,16},{16,24},{24,32},{32,40},{40,48},{48,56},{56,0},{1,9},... | collective-permute-start | bytes 688136 | tf_op jit(solution)/shard_map/reduce/ppermute | solution.py:386
  119.6 3.6 %collective-permute-start.80 = (bf16[128,896]{1,0:T(8,128)(2,1)S(1)}, bf16[128,896]{1,0:T(8,128)(2,1)S(1)}, u32[]{:S(2)}, u32[]{:S(2)}) collective-permute-start(bf16[128,896]{1,0:T(8,128)(2,1)S(1)} %get-tuple-element.154), channel_id=1, source_target_pairs={{0,64},{64,128},{128,192},{192,0},{1,65},{65,129},{129,193},{193,1... | collective-permute-start | bytes 688136 | tf_op jit(solution)/shard_map/reduce/ppermute | solution.py:386
  125.2 4.7 %collective-permute-done.80 = bf16[128,896]{1,0:T(8,128)(2,1)S(1)} collective-permute-done((bf16[128,896]{1,0:T(8,128)(2,1)S(1)}, bf16[128,896]{1,0:T(8,128)(2,1)S(1)}, u32[]{:S(2)}, u32[]{:S(2)}) %collective-permute-start.80) | collective-permute-done | bytes 229408 | tf_op jit(solution)/shard_map/reduce/ppermute | solution.py:386
  131.2 2.2 %collective-permute-done.82 = bf16[128,896]{1,0:T(8,128)(2,1)S(1)} collective-permute-done((bf16[128,896]{1,0:T(8,128)(2,1)S(1)}, bf16[128,896]{1,0:T(8,128)(2,1)S(1)}, u32[]{:S(2)}, u32[]{:S(2)}) %collective-permute-start.82) | collective-permute-done | bytes 229408 | tf_op jit(solution)/shard_map/reduce/ppermute | solution.py:386
  (69 shorter events, 29.2 us)
Async XLA Ops:
  0.6 11.7 %collective-permute-start.44 = (bf16[128,896]{1,0:T(8,128)(2,1)}, bf16[128,896]{1,0:T(8,128)(2,1)S(1)}, u32[]{:S(2)}, u32[]{:S(2)}) collective-permute-start(bf16[128,896]{1,0:T(8,128)(2,1)} %refs_0_.3), channel_id=1, source_target_pairs={{0,8},{8,16},{16,24},{24,32},{32,40},{40,48},{48,56},{56,0},{1,9},... | collective-permute-start | bytes 688136 | tf_op jit(solution)/shard_map/gather/ppermute | solution.py:386
  2.6 9.8 %collective-permute-start.45 = (bf16[128,896]{1,0:T(8,128)(2,1)}, bf16[128,896]{1,0:T(8,128)(2,1)S(1)}, u32[]{:S(2)}, u32[]{:S(2)}) collective-permute-start(bf16[128,896]{1,0:T(8,128)(2,1)} %refs_0_.3), channel_id=1, source_target_pairs={{0,56},{8,0},{16,8},{24,16},{32,24},{40,32},{48,40},{56,48},{1,57}... | collective-permute-start | bytes 688136 | tf_op jit(solution)/shard_map/gather/ppermute | solution.py:386
  12.4 8.0 %collective-permute-start.48 = (bf16[128,896]{1,0:T(8,128)(2,1)S(1)}, bf16[128,896]{1,0:T(8,128)(2,1)S(1)}, u32[]{:S(2)}, u32[]{:S(2)}) collective-permute-start(bf16[128,896]{1,0:T(8,128)(2,1)S(1)} %collective-permute-done.44.refs_4_), channel_id=1, source_target_pairs={{0,8},{8,16},{16,24},{24,32},{32,40},{40,48},{48,56},{56,0},{1,9},... | collective-permute-start | bytes 688136 | tf_op jit(solution)/shard_map/gather/ppermute | solution.py:386
  12.4 8.0 %collective-permute-start.46 = (bf16[128,896]{1,0:T(8,128)(2,1)S(1)}, bf16[128,896]{1,0:T(8,128)(2,1)S(1)}, u32[]{:S(2)}, u32[]{:S(2)}) collective-permute-start(bf16[128,896]{1,0:T(8,128)(2,1)S(1)} %collective-permute-done.45.refs_1_), channel_id=1, source_target_pairs={{0,56},{8,0},{16,8},{24,16},{32,24},{40,32},{48,40},{56,48},{1,57}... | collective-permute-start | bytes 688136 | tf_op jit(solution)/shard_map/gather/ppermute | solution.py:386
  15.6 12.6 %collective-permute-start.53 = (bf16[128,896]{1,0:T(8,128)(2,1)}, bf16[128,896]{1,0:T(8,128)(2,1)S(1)}, u32[]{:S(2)}, u32[]{:S(2)}) collective-permute-start(bf16[128,896]{1,0:T(8,128)(2,1)} %refs_4_.1), channel_id=1, source_target_pairs={{0,192},{64,0},{128,64},{192,128},{1,193},{65,1},{129,65},{193,129... | collective-permute-start | bytes 688136 | tf_op jit(solution)/shard_map/gather/ppermute | solution.py:386
  16.4 11.8 %collective-permute-start.55 = (bf16[128,896]{1,0:T(8,128)(2,1)}, bf16[128,896]{1,0:T(8,128)(2,1)S(1)}, u32[]{:S(2)}, u32[]{:S(2)}) collective-permute-start(bf16[128,896]{1,0:T(8,128)(2,1)} %refs_4_.1), channel_id=1, source_target_pairs={{0,128},{64,192},{128,0},{192,64},{1,129},{65,193},{129,1},{193,65... | collective-permute-start | bytes 688136 | tf_op jit(solution)/shard_map/gather/ppermute | solution.py:386
  17.3 11.5 %collective-permute-start.57 = (bf16[128,896]{1,0:T(8,128)(2,1)}, bf16[128,896]{1,0:T(8,128)(2,1)S(1)}, u32[]{:S(2)}, u32[]{:S(2)}) collective-permute-start(bf16[128,896]{1,0:T(8,128)(2,1)} %refs_4_.1), channel_id=1, source_target_pairs={{0,64},{64,128},{128,192},{192,0},{1,65},{65,129},{129,193},{193,1... | collective-permute-start | bytes 688136 | tf_op jit(solution)/shard_map/gather/ppermute | solution.py:386
  20.4 8.4 %collective-permute-start.49 = (bf16[128,896]{1,0:T(8,128)(2,1)S(1)}, bf16[128,896]{1,0:T(8,128)(2,1)S(1)}, u32[]{:S(2)}, u32[]{:S(2)}) collective-permute-start(bf16[128,896]{1,0:T(8,128)(2,1)S(1)} %collective-permute-done.48.refs_5_), channel_id=1, source_target_pairs={{0,8},{8,16},{16,24},{24,32},{32,40},{40,48},{48,56},{56,0},{1,9},... | collective-permute-start | bytes 688136 | tf_op jit(solution)/shard_map/gather/ppermute | solution.py:386
  20.4 8.9 %collective-permute-start.47 = (bf16[128,896]{1,0:T(8,128)(2,1)S(1)}, bf16[128,896]{1,0:T(8,128)(2,1)S(1)}, u32[]{:S(2)}, u32[]{:S(2)}) collective-permute-start(bf16[128,896]{1,0:T(8,128)(2,1)S(1)} %collective-permute-done.46.refs_2_), channel_id=1, source_target_pairs={{0,56},{8,0},{16,8},{24,16},{32,24},{40,32},{48,40},{56,48},{1,57}... | collective-permute-start | bytes 688136 | tf_op jit(solution)/shard_map/gather/ppermute | solution.py:386
  29.4 6.4 %collective-permute-start.50 = (bf16[64,896]{1,0:T(8,128)(2,1)S(1)}, bf16[64,896]{1,0:T(8,128)(2,1)S(1)}, u32[]{:S(2)}, u32[]{:S(2)}) collective-permute-start(bf16[64,896]{1,0:T(8,128)(2,1)S(1)} %slice.24), channel_id=1, source_target_pairs={{0,8},{8,16},{16,24},{24,32},{32,40},{40,48},{48,56},{56,0},{1,9},... | collective-permute-start | bytes 344072 | tf_op jit(solution)/shard_map/gather/ppermute | solution.py:386
  30.1 5.6 %collective-permute-start.51 = (bf16[64,896]{1,0:T(8,128)(2,1)S(1)}, bf16[64,896]{1,0:T(8,128)(2,1)S(1)}, u32[]{:S(2)}, u32[]{:S(2)}) collective-permute-start(bf16[64,896]{1,0:T(8,128)(2,1)S(1)} %slice.25), channel_id=1, source_target_pairs={{0,56},{8,0},{16,8},{24,16},{32,24},{40,32},{48,40},{56,48},{1,57}... | collective-permute-start | bytes 344072 | tf_op jit(solution)/shard_map/gather/ppermute | solution.py:386
  38.5 10.2 %collective-permute-start.59 = (f32[18,32,128]{2,1,0:T(8,128)S(1)}, f32[18,32,128]{2,1,0:T(8,128)S(1)}, u32[]{:S(2)}, u32[]{:S(2)}) collective-permute-start(f32[18,32,128]{2,1,0:T(8,128)S(1)} %get-tuple-element.124), channel_id=1, source_target_pairs={{0,1},{1,2},{2,3},{3,0},{4,5},{5,6},{6,7},{7,4},{8,9},{9,10},{10,1... | collective-permute-start | bytes 884744 | tf_op jit(solution)/shard_map/scores_over_x/ppermute | solution.py:386
  40.1 15.1 %collective-permute-start.60 = (f32[18,32,128]{2,1,0:T(8,128)S(1)}, f32[18,32,128]{2,1,0:T(8,128)S(1)}, u32[]{:S(2)}, u32[]{:S(2)}) collective-permute-start(f32[18,32,128]{2,1,0:T(8,128)S(1)} %get-tuple-element.125), channel_id=1, source_target_pairs={{0,2},{1,3},{2,0},{3,1},{4,6},{5,7},{6,4},{7,5},{8,10},{9,11},{10,... | collective-permute-start | bytes 884744 | tf_op jit(solution)/shard_map/scores_over_x/ppermute | solution.py:386
  42.9 12.4 %collective-permute-start.61 = (f32[18,32,128]{2,1,0:T(8,128)S(1)}, f32[18,32,128]{2,1,0:T(8,128)S(1)}, u32[]{:S(2)}, u32[]{:S(2)}) collective-permute-start(f32[18,32,128]{2,1,0:T(8,128)S(1)} %get-tuple-element.126), channel_id=1, source_target_pairs={{0,3},{1,0},{2,1},{3,2},{4,7},{5,4},{6,5},{7,6},{8,11},{9,8},{10,9... | collective-permute-start | bytes 884744 | tf_op jit(solution)/shard_map/scores_over_x/ppermute | solution.py:386
  60.4 4.9 %collective-permute-start.64 = (f32[2,32,128]{2,1,0:T(8,128)S(1)}, f32[2,32,128]{2,1,0:T(8,128)S(1)}, u32[]{:S(2)}, u32[]{:S(2)}) collective-permute-start(f32[2,32,128]{2,1,0:T(8,128)S(1)} %get-tuple-element.129.refs_0_), channel_id=1, source_target_pairs={{0,16},{8,24},{16,0},{24,8},{32,48},{40,56},{48,32},{56,40},{1,17}... | collective-permute-start | bytes 98312 | tf_op jit(solution)/shard_map/stats/ppermute | solution.py:416
  66.8 7.9 %collective-permute-start.66 = (f32[2,32,128]{2,1,0:T(8,128)S(1)}, f32[2,32,128]{2,1,0:T(8,128)S(1)}, u32[]{:S(2)}, u32[]{:S(2)}) collective-permute-start(f32[2,32,128]{2,1,0:T(8,128)S(1)} %get-tuple-element.131.za), channel_id=1, source_target_pairs={{0,32},{8,40},{16,48},{24,56},{32,0},{40,8},{48,16},{56,24},{1,33}... | collective-permute-start | bytes 98312 | tf_op jit(solution)/shard_map/stats/ppermute | solution.py:416
  69.1 5.6 %collective-permute-start.67 = (f32[2,32,128]{2,1,0:T(8,128)S(1)}, f32[2,32,128]{2,1,0:T(8,128)S(1)}, u32[]{:S(2)}, u32[]{:S(2)}) collective-permute-start(f32[2,32,128]{2,1,0:T(8,128)S(1)} %get-tuple-element.132.ya), channel_id=1, source_target_pairs={{0,128},{64,192},{128,0},{192,64},{1,129},{65,193},{129,1},{193,65... | collective-permute-start | bytes 98312 | tf_op jit(solution)/shard_map/stats/ppermute | solution.py:416
  75.7 6.8 %collective-permute-start.68 = (bf16[18,32,128]{2,1,0:T(8,128)(2,1)S(1)}, bf16[18,32,128]{2,1,0:T(8,128)(2,1)S(1)}, u32[]{:S(2)}, u32[]{:S(2)}) collective-permute-start(bf16[18,32,128]{2,1,0:T(8,128)(2,1)S(1)} %coefficients.1.refs_0_), channel_id=1, source_target_pairs={{0,3},{1,0},{2,1},{3,2},{4,7},{5,4},{6,5},{7,6},{8,11},{9,8},{10,9... | collective-permute-start | bytes 442376 | tf_op jit(solution)/shard_map/coefs_over_x/ppermute | solution.py:386
  78.2 6.7 %collective-permute-start.69 = (bf16[18,32,128]{2,1,0:T(8,128)(2,1)S(1)}, bf16[18,32,128]{2,1,0:T(8,128)(2,1)S(1)}, u32[]{:S(2)}, u32[]{:S(2)}) collective-permute-start(bf16[18,32,128]{2,1,0:T(8,128)(2,1)S(1)} %coefficients.1.refs_0_), channel_id=1, source_target_pairs={{0,2},{1,3},{2,0},{3,1},{4,6},{5,7},{6,4},{7,5},{8,10},{9,11},{10,... | collective-permute-start | bytes 442376 | tf_op jit(solution)/shard_map/coefs_over_x/ppermute | solution.py:386
  79.3 7.1 %collective-permute-start.70 = (bf16[18,32,128]{2,1,0:T(8,128)(2,1)S(1)}, bf16[18,32,128]{2,1,0:T(8,128)(2,1)S(1)}, u32[]{:S(2)}, u32[]{:S(2)}) collective-permute-start(bf16[18,32,128]{2,1,0:T(8,128)(2,1)S(1)} %coefficients.1.refs_0_), channel_id=1, source_target_pairs={{0,1},{1,2},{2,3},{3,0},{4,5},{5,6},{6,7},{7,4},{8,9},{9,10},{10,1... | collective-permute-start | bytes 442376 | tf_op jit(solution)/shard_map/coefs_over_x/ppermute | solution.py:386
  92.4 27.0 %collective-permute-start.79 = (bf16[4,128,896]{2,1,0:T(8,128)(2,1)S(1)}, bf16[4,128,896]{2,1,0:T(8,128)(2,1)S(1)}, u32[]{:S(2)}, u32[]{:S(2)}) collective-permute-start(bf16[4,128,896]{2,1,0:T(8,128)(2,1)S(1)} %get-tuple-element.150), channel_id=1, source_target_pairs={{0,4},{4,0},{1,5},{5,1},{2,6},{6,2},{3,7},{7,3},{8,12},{12,8},{9,1... | collective-permute-start | bytes 2752520 | tf_op jit(solution)/shard_map/reduce/ppermute | solution.py:386
  92.5 6.9 %collective-permute-start.71 = (bf16[64,896]{1,0:T(8,128)(2,1)S(1)}, bf16[64,896]{1,0:T(8,128)(2,1)S(1)}, u32[]{:S(2)}, u32[]{:S(2)}) collective-permute-start(bf16[64,896]{1,0:T(8,128)(2,1)S(1)} %get-tuple-element.134), channel_id=1, source_target_pairs={{0,8},{8,16},{16,24},{24,32},{32,40},{40,48},{48,56},{56,0},{1,9},... | collective-permute-start | bytes 344072 | tf_op jit(solution)/shard_map/reduce/ppermute | solution.py:386
  92.6 6.8 %collective-permute-start.72 = (bf16[64,896]{1,0:T(8,128)(2,1)S(1)}, bf16[64,896]{1,0:T(8,128)(2,1)S(1)}, u32[]{:S(2)}, u32[]{:S(2)}) collective-permute-start(bf16[64,896]{1,0:T(8,128)(2,1)S(1)} %get-tuple-element.135), channel_id=1, source_target_pairs={{0,56},{8,0},{16,8},{24,16},{32,24},{40,32},{48,40},{56,48},{1,57}... | collective-permute-start | bytes 344072 | tf_op jit(solution)/shard_map/reduce/ppermute | solution.py:386
  99.5 8.6 %collective-permute-start.73 = (bf16[128,896]{1,0:T(8,128)(2,1)S(1)}, bf16[128,896]{1,0:T(8,128)(2,1)S(1)}, u32[]{:S(2)}, u32[]{:S(2)}) collective-permute-start(bf16[128,896]{1,0:T(8,128)(2,1)S(1)} %get-tuple-element.138), channel_id=1, source_target_pairs={{0,8},{8,16},{16,24},{24,32},{32,40},{40,48},{48,56},{56,0},{1,9},... | collective-permute-start | bytes 688136 | tf_op jit(solution)/shard_map/reduce/ppermute | solution.py:386
  99.7 8.4 %collective-permute-start.74 = (bf16[128,896]{1,0:T(8,128)(2,1)S(1)}, bf16[128,896]{1,0:T(8,128)(2,1)S(1)}, u32[]{:S(2)}, u32[]{:S(2)}) collective-permute-start(bf16[128,896]{1,0:T(8,128)(2,1)S(1)} %get-tuple-element.139), channel_id=1, source_target_pairs={{0,56},{8,0},{16,8},{24,16},{32,24},{40,32},{48,40},{56,48},{1,57}... | collective-permute-start | bytes 688136 | tf_op jit(solution)/shard_map/reduce/ppermute | solution.py:386
  108.2 7.7 %collective-permute-start.75 = (bf16[128,896]{1,0:T(8,128)(2,1)S(1)}, bf16[128,896]{1,0:T(8,128)(2,1)S(1)}, u32[]{:S(2)}, u32[]{:S(2)}) collective-permute-start(bf16[128,896]{1,0:T(8,128)(2,1)S(1)} %get-tuple-element.142), channel_id=1, source_target_pairs={{0,8},{8,16},{16,24},{24,32},{32,40},{40,48},{48,56},{56,0},{1,9},... | collective-permute-start | bytes 688136 | tf_op jit(solution)/shard_map/reduce/ppermute | solution.py:386
  109.5 6.5 %collective-permute-start.76 = (bf16[128,896]{1,0:T(8,128)(2,1)S(1)}, bf16[128,896]{1,0:T(8,128)(2,1)S(1)}, u32[]{:S(2)}, u32[]{:S(2)}) collective-permute-start(bf16[128,896]{1,0:T(8,128)(2,1)S(1)} %get-tuple-element.143), channel_id=1, source_target_pairs={{0,56},{8,0},{16,8},{24,16},{32,24},{40,32},{48,40},{56,48},{1,57}... | collective-permute-start | bytes 688136 | tf_op jit(solution)/shard_map/reduce/ppermute | solution.py:386
  116.1 8.1 %collective-permute-start.77 = (bf16[128,896]{1,0:T(8,128)(2,1)S(1)}, bf16[128,896]{1,0:T(8,128)(2,1)S(1)}, u32[]{:S(2)}, u32[]{:S(2)}) collective-permute-start(bf16[128,896]{1,0:T(8,128)(2,1)S(1)} %get-tuple-element.146), channel_id=1, source_target_pairs={{0,8},{8,16},{16,24},{24,32},{32,40},{40,48},{48,56},{56,0},{1,9},... | collective-permute-start | bytes 688136 | tf_op jit(solution)/shard_map/reduce/ppermute | solution.py:386
  118.3 6.0 %collective-permute-start.78 = (bf16[128,896]{1,0:T(8,128)(2,1)S(1)}, bf16[128,896]{1,0:T(8,128)(2,1)S(1)}, u32[]{:S(2)}, u32[]{:S(2)}) collective-permute-start(bf16[128,896]{1,0:T(8,128)(2,1)S(1)} %get-tuple-element.147), channel_id=1, source_target_pairs={{0,56},{8,0},{16,8},{24,16},{32,24},{40,32},{48,40},{56,48},{1,57}... | collective-permute-start | bytes 688136 | tf_op jit(solution)/shard_map/reduce/ppermute | solution.py:386
  119.6 10.3 %collective-permute-start.80 = (bf16[128,896]{1,0:T(8,128)(2,1)S(1)}, bf16[128,896]{1,0:T(8,128)(2,1)S(1)}, u32[]{:S(2)}, u32[]{:S(2)}) collective-permute-start(bf16[128,896]{1,0:T(8,128)(2,1)S(1)} %get-tuple-element.154), channel_id=1, source_target_pairs={{0,64},{64,128},{128,192},{192,0},{1,65},{65,129},{129,193},{193,1... | collective-permute-start | bytes 688136 | tf_op jit(solution)/shard_map/reduce/ppermute | solution.py:386
  123.2 8.1 %collective-permute-start.81 = (bf16[128,896]{1,0:T(8,128)(2,1)S(1)}, bf16[128,896]{1,0:T(8,128)(2,1)S(1)}, u32[]{:S(2)}, u32[]{:S(2)}) collective-permute-start(bf16[128,896]{1,0:T(8,128)(2,1)S(1)} %get-tuple-element.155), channel_id=1, source_target_pairs={{0,128},{64,192},{128,0},{192,64},{1,129},{65,193},{129,1},{193,65... | collective-permute-start | bytes 688136 | tf_op jit(solution)/shard_map/reduce/ppermute | solution.py:386
  123.5 10.0 %collective-permute-start.82 = (bf16[128,896]{1,0:T(8,128)(2,1)S(1)}, bf16[128,896]{1,0:T(8,128)(2,1)S(1)}, u32[]{:S(2)}, u32[]{:S(2)}) collective-permute-start(bf16[128,896]{1,0:T(8,128)(2,1)S(1)} %get-tuple-element.156), channel_id=1, source_target_pairs={{0,192},{64,0},{128,64},{192,128},{1,193},{65,1},{129,65},{193,129... | collective-permute-start | bytes 688136 | tf_op jit(solution)/shard_map/reduce/ppermute | solution.py:386
  (10 other events, 82.3 us)
where the time goes:
time: 136 us; the launch traced here: 135 us
  waiting for transfers between devices  62.8 us (46%)
  starting transfers between devices  55.6 us (41%)
  Pallas kernels  13.3 us (10%)
  other arithmetic  1.73 us (1%)
    ppermute x33, waiting for transfers between devices, shift(): return lax.ppermute(value, axis, [(i, (i + by) % n) for i in range(n)])  52 us
    ppermute x33, starting transfers between devices, shift(): return lax.ppermute(value, axis, [(i, (i + by) % n) for i in range(n)])  48.2 us
    ppermute x6, waiting for transfers between devices, swap(): return lax.ppermute(value, axis, [(i, i ^ bit) for i in range(n)])  10.9 us
    ppermute x6, starting transfers between devices, swap(): return lax.ppermute(value, axis, [(i, i ^ bit) for i in range(n)])  7.46 us
    pallas_call x1, Pallas kernels, query_grads(): pl.pallas_call(query_grad_kernel, out_shape=[jax.ShapeDtypeStruct((cap, B...  3.03 us
    pallas_call x1, Pallas kernels, code_grads(): pl.pallas_call(code_grad_kernel, out_shape=[jax.ShapeDtypeStruct((BLK, fe...  2.92 us
    pallas_call x1, Pallas kernels, partial_scores(): pl.pallas_call(score_kernel, out_shape=[jax.ShapeDtypeStruct((cap, QUARTE...  2.78 us
  transfers between devices with their start and end apart: 39, of which 22 were waited for; matrix products, arithmetic and copies ran while one was open for 1% of the time, Pallas kernels for 2%

commit v1 on v0

--- a/solution.py
+++ b/solution.py
@@ -461,14 +461,16 @@
     return [total(part, other[d + 1]).astype(BF16) for d, part in enumerate(parts)]
 
 
-def reduce_queries(g, p1, p2, p3, p4a, p4b, m1, m2, m3):
+def reduce_queries(early, p1, p2, p3, p4a, p4b, m1, m2, m3):
     like = [jax.ShapeDtypeStruct(p1.shape, BF16)] * 2
     r, l = shift(p4a, "z", 1), shift(p4b, "z", -1)
     r, l = small_kernel(join_halves, "join_halves", like, r, l, p3, m3)
     for a, b in ((p2, m2), (p1, m1)):
         r, l = shift(r, "z", 1), shift(l, "z", -1)
+        if a is p1:
+            r, l, early = lax.optimization_barrier((r, l, early))
         r, l = small_kernel(join, "join", like, r, l, a, b)
-    return (shift(r, "z", 1), shift(l, "z", -1)), g
+    return (shift(r, "z", 1), shift(l, "z", -1)), early
 
 
 def reduce_codes(po, *parts):
@@ -493,9 +495,9 @@
         coefs = (coefs, *from_others(coefs, "x"))
     g, own_q, *parts = query_grads(cap, ent, coefs, c_parts)
     with jax.named_scope("reduce"):
-        from_z, g = reduce_queries(g, *parts)
         own_c, pc1, pc2, pc3, po = code_grads(ent, g, q_parts)
         from_yc = reduce_codes(po, pc1, pc2, pc3)
+        from_z, from_yc = reduce_queries(from_yc, *parts)
     return over, (total(own_q, *from_z), total(own_c, *from_yc))
 
 

time: 136 us -> 139 us (1.022)
  waiting for transfers between devices: 62.8 us -> 65.5 us
    ppermute x33, waiting for transfers between devices: 52 us -> 54.4 us  [shift(): return lax.ppermute(value, axis, [(i, (i + by) % n) for i in range(n)])]
  transfers between devices with their start and end apart: 39 -> 39, of which waited for: 22 -> 25; matrix products, arithmetic and copies ran while one was open for 1% -> 1% of each run, Pallas kernels for 2% -> 2%
where the time goes in v1:
time: 139 us; the launch traced here: 138 us
  waiting for transfers between devices  65.5 us (47%)
  starting transfers between devices  56.4 us (41%)
  Pallas kernels  12.5 us (9%)
  other arithmetic  1.75 us (1%)
    ppermute x33, waiting for transfers between devices, shift(): return lax.ppermute(value, axis, [(i, (i + by) % n) for i in range(n)])  54.4 us
    ppermute x33, starting transfers between devices, shift(): return lax.ppermute(value, axis, [(i, (i + by) % n) for i in range(n)])  48 us
    ppermute x6, waiting for transfers between devices, swap(): return lax.ppermute(value, axis, [(i, i ^ bit) for i in range(n)])  11.1 us
    ppermute x6, starting transfers between devices, swap(): return lax.ppermute(value, axis, [(i, i ^ bit) for i in range(n)])  8.45 us
  transfers between devices with their start and end apart: 39, of which 25 were waited for; matrix products, arithmetic and copies ran while one was open for 1% of the time, Pallas kernels for 2%

profile of v1, /device:TPU:24, one launch (start us, length us, event | category | flops | bytes accessed | tf_op | source)
XLA Modules:
  0.0 138.1 jit_solution(12564134647969741572)
XLA Ops:
  0.6 2.0 %collective-permute-start.44 = (bf16[128,896]{1,0:T(8,128)(2,1)}, bf16[128,896]{1,0:T(8,128)(2,1)S(1)}, u32[]{:S(2)}, u32[]{:S(2)}) collective-permute-start(bf16[128,896]{1,0:T(8,128)(2,1)} %refs_0_.3), channel_id=1, source_target_pairs={{0,8},{8,16},{16,24},{24,32},{32,40},{40,48},{48,56},{56,0},{1,9},... | collective-permute-start | bytes 688136 | tf_op jit(solution)/shard_map/gather/ppermute | solution.py:386
  2.6 4.0 %collective-permute-start.45 = (bf16[128,896]{1,0:T(8,128)(2,1)}, bf16[128,896]{1,0:T(8,128)(2,1)S(1)}, u32[]{:S(2)}, u32[]{:S(2)}) collective-permute-start(bf16[128,896]{1,0:T(8,128)(2,1)} %refs_0_.3), channel_id=1, source_target_pairs={{0,56},{8,0},{16,8},{24,16},{32,24},{40,32},{48,40},{56,48},{1,57}... | collective-permute-start | bytes 688136 | tf_op jit(solution)/shard_map/gather/ppermute | solution.py:386
  6.7 2.1 %block_list.3 = (s32[3,88]{1,0:T(4,128)S(1)}, s32[1]{0:T(128)}) custom-call(s32[4,64]{1,0:T(4,128)} %bitcast.12, s32[64]{0:T(128)} %count_ref.1, s32[4,64]{1,0:T(4,128)} %bitcast.13, s32[1,64]{1,0:T(1,128)} %bitcast.16), custom_call_target="tpu_custom_call" | custom-call | tf_op jit(solution)/shard_map/block_list/pallas_call | solution.py:100
  8.7 3.6 %collective-permute-done.44.refs_4_ = bf16[128,896]{1,0:T(8,128)(2,1)S(1)} collective-permute-done((bf16[128,896]{1,0:T(8,128)(2,1)}, bf16[128,896]{1,0:T(8,128)(2,1)S(1)}, u32[]{:S(2)}, u32[]{:S(2)}) %collective-permute-start.44) | collective-permute-done | bytes 229408 | tf_op jit(solution)/shard_map/gather/ppermute | solution.py:386
  12.4 3.2 %collective-permute-start.46 = (bf16[128,896]{1,0:T(8,128)(2,1)S(1)}, bf16[128,896]{1,0:T(8,128)(2,1)S(1)}, u32[]{:S(2)}, u32[]{:S(2)}) collective-permute-start(bf16[128,896]{1,0:T(8,128)(2,1)S(1)} %collective-permute-done.45.refs_1_), channel_id=1, source_target_pairs={{0,56},{8,0},{16,8},{24,16},{32,24},{40,32},{48,40},{56,48},{1,57}... | collective-permute-start | bytes 688136 | tf_op jit(solution)/shard_map/gather/ppermute | solution.py:386
  17.3 2.2 %collective-permute-start.57 = (bf16[128,896]{1,0:T(8,128)(2,1)}, bf16[128,896]{1,0:T(8,128)(2,1)S(1)}, u32[]{:S(2)}, u32[]{:S(2)}) collective-permute-start(bf16[128,896]{1,0:T(8,128)(2,1)} %refs_4_.1), channel_id=1, source_target_pairs={{0,64},{64,128},{128,192},{192,0},{1,65},{65,129},{129,193},{193,1... | collective-permute-start | bytes 688136 | tf_op jit(solution)/shard_map/gather/ppermute | solution.py:386
  20.4 3.2 %collective-permute-start.47 = (bf16[128,896]{1,0:T(8,128)(2,1)S(1)}, bf16[128,896]{1,0:T(8,128)(2,1)S(1)}, u32[]{:S(2)}, u32[]{:S(2)}) collective-permute-start(bf16[128,896]{1,0:T(8,128)(2,1)S(1)} %collective-permute-done.46.refs_2_), channel_id=1, source_target_pairs={{0,56},{8,0},{16,8},{24,16},{32,24},{40,32},{48,40},{56,48},{1,57}... | collective-permute-start | bytes 688136 | tf_op jit(solution)/shard_map/gather/ppermute | solution.py:386
  23.6 4.6 %collective-permute-done.53.refs_11_.refs_6_ = bf16[128,896]{1,0:T(8,128)(2,1)S(1)} collective-permute-done((bf16[128,896]{1,0:T(8,128)(2,1)}, bf16[128,896]{1,0:T(8,128)(2,1)S(1)}, u32[]{:S(2)}, u32[]{:S(2)}) %collective-permute-start.53) | collective-permute-done | bytes 229408 | tf_op jit(solution)/shard_map/gather/ppermute | solution.py:386
  30.1 2.5 %collective-permute-start.51 = (bf16[64,896]{1,0:T(8,128)(2,1)S(1)}, bf16[64,896]{1,0:T(8,128)(2,1)S(1)}, u32[]{:S(2)}, u32[]{:S(2)}) collective-permute-start(bf16[64,896]{1,0:T(8,128)(2,1)S(1)} %slice.25), channel_id=1, source_target_pairs={{0,56},{8,0},{16,8},{24,16},{32,24},{40,32},{48,40},{56,48},{1,57}... | collective-permute-start | bytes 344072 | tf_op jit(solution)/shard_map/gather/ppermute | solution.py:386
  32.7 3.0 %collective-permute-done.50.refs_7_ = bf16[64,896]{1,0:T(8,128)(2,1)S(1)} collective-permute-done((bf16[64,896]{1,0:T(8,128)(2,1)S(1)}, bf16[64,896]{1,0:T(8,128)(2,1)S(1)}, u32[]{:S(2)}, u32[]{:S(2)}) %collective-permute-start.50) | collective-permute-done | bytes 114720 | tf_op jit(solution)/shard_map/gather/ppermute | solution.py:386
  35.7 2.5 %scores.3 = (f32[18,32,128]{2,1,0:T(8,128)S(1)}, f32[18,32,128]{2,1,0:T(8,128)S(1)}, f32[18,32,128]{2,1,0:T(8,128)S(1)}, f32[18,32,128]{2,1,0:T(8,128)S(1)}) custom-call(s32[3,88]{1,0:T(4,128)S(1)} %get-tuple-element.128.ent, bf16[128,896]{1,0:T(8,128)(2,1)} %refs_0_.3, bf16[128,896]{1,0:T(8,128)(2,1)S(1)} %collective-permute-done.45.refs_1_, ...), custom_call_target="tpu_custom_call" | custom-call | tf_op jit(solution)/shard_map/scores/pallas_call | solution.py:169
  39.9 2.7 %collective-permute-start.60 = (f32[18,32,128]{2,1,0:T(8,128)S(1)}, f32[18,32,128]{2,1,0:T(8,128)S(1)}, u32[]{:S(2)}, u32[]{:S(2)}) collective-permute-start(f32[18,32,128]{2,1,0:T(8,128)S(1)} %get-tuple-element.133), channel_id=1, source_target_pairs={{0,2},{1,3},{2,0},{3,1},{4,6},{5,7},{6,4},{7,5},{8,10},{9,11},{10,... | collective-permute-start | bytes 884744 | tf_op jit(solution)/shard_map/scores_over_x/ppermute | solution.py:386
  44.0 4.5 %collective-permute-done.59.s1 = f32[18,32,128]{2,1,0:T(8,128)S(1)} collective-permute-done((f32[18,32,128]{2,1,0:T(8,128)S(1)}, f32[18,32,128]{2,1,0:T(8,128)S(1)}, u32[]{:S(2)}, u32[]{:S(2)}) %collective-permute-start.59) | collective-permute-done | bytes 294944 | tf_op jit(solution)/shard_map/scores_over_x/ppermute | solution.py:386
  48.6 6.2 %collective-permute-done.60.s2 = f32[18,32,128]{2,1,0:T(8,128)S(1)} collective-permute-done((f32[18,32,128]{2,1,0:T(8,128)S(1)}, f32[18,32,128]{2,1,0:T(8,128)S(1)}, u32[]{:S(2)}, u32[]{:S(2)}) %collective-permute-start.60) | collective-permute-done | bytes 294944 | tf_op jit(solution)/shard_map/scores_over_x/ppermute | solution.py:386
  56.5 3.3 %collective-permute-done.62.refs_1_ = f32[2,32,128]{2,1,0:T(8,128)S(1)} collective-permute-done((f32[2,32,128]{2,1,0:T(8,128)S(1)}, f32[2,32,128]{2,1,0:T(8,128)S(1)}, u32[]{:S(2)}, u32[]{:S(2)}) %collective-permute-start.62) | collective-permute-done | bytes 32800 | tf_op jit(solution)/shard_map/stats/ppermute | solution.py:416
  59.8 3.0 %collective-permute-start.64 = (f32[2,32,128]{2,1,0:T(8,128)S(1)}, f32[2,32,128]{2,1,0:T(8,128)S(1)}, u32[]{:S(2)}, u32[]{:S(2)}) collective-permute-start(f32[2,32,128]{2,1,0:T(8,128)S(1)} %get-tuple-element.137.refs_0_), channel_id=1, source_target_pairs={{0,16},{8,24},{16,0},{24,8},{32,48},{40,56},{48,32},{56,40},{1,17}... | collective-permute-start | bytes 98312 | tf_op jit(solution)/shard_map/stats/ppermute | solution.py:416
  66.8 3.3 %collective-permute-start.66 = (f32[2,32,128]{2,1,0:T(8,128)S(1)}, f32[2,32,128]{2,1,0:T(8,128)S(1)}, u32[]{:S(2)}, u32[]{:S(2)}) collective-permute-start(f32[2,32,128]{2,1,0:T(8,128)S(1)} %get-tuple-element.139.za), channel_id=1, source_target_pairs={{0,32},{8,40},{16,48},{24,56},{32,0},{40,8},{48,16},{56,24},{1,33}... | collective-permute-start | bytes 98312 | tf_op jit(solution)/shard_map/stats/ppermute | solution.py:416
  71.4 3.2 %collective-permute-done.66.zb = f32[2,32,128]{2,1,0:T(8,128)S(1)} collective-permute-done((f32[2,32,128]{2,1,0:T(8,128)S(1)}, f32[2,32,128]{2,1,0:T(8,128)S(1)}, u32[]{:S(2)}, u32[]{:S(2)}) %collective-permute-start.66) | collective-permute-done | bytes 32800 | tf_op jit(solution)/shard_map/stats/ppermute | solution.py:416
  76.4 2.5 %collective-permute-start.68 = (bf16[18,32,128]{2,1,0:T(8,128)(2,1)S(1)}, bf16[18,32,128]{2,1,0:T(8,128)(2,1)S(1)}, u32[]{:S(2)}, u32[]{:S(2)}) collective-permute-start(bf16[18,32,128]{2,1,0:T(8,128)(2,1)S(1)} %coefficients.1.refs_0_), channel_id=1, source_target_pairs={{0,3},{1,0},{2,1},{3,2},{4,7},{5,4},{6,5},{7,6},{8,11},{9,8},{10,9... | collective-permute-start | bytes 442376 | tf_op jit(solution)/shard_map/coefs_over_x/ppermute | solution.py:386
  80.5 2.6 %collective-permute-done.68.refs_1_ = bf16[18,32,128]{2,1,0:T(8,128)(2,1)S(1)} collective-permute-done((bf16[18,32,128]{2,1,0:T(8,128)(2,1)S(1)}, bf16[18,32,128]{2,1,0:T(8,128)(2,1)S(1)}, u32[]{:S(2)}, u32[]{:S(2)}) %collective-permute-start.68) | collective-permute-done | bytes 147488 | tf_op jit(solution)/shard_map/coefs_over_x/ppermute | solution.py:386
  83.2 2.4 %collective-permute-done.69.refs_2_ = bf16[18,32,128]{2,1,0:T(8,128)(2,1)S(1)} collective-permute-done((bf16[18,32,128]{2,1,0:T(8,128)(2,1)S(1)}, bf16[18,32,128]{2,1,0:T(8,128)(2,1)S(1)}, u32[]{:S(2)}, u32[]{:S(2)}) %collective-permute-start.69) | collective-permute-done | bytes 147488 | tf_op jit(solution)/shard_map/coefs_over_x/ppermute | solution.py:386
  87.1 2.8 %query_grads.3 = (bf16[18,128,128]{2,1,0:T(8,128)(2,1)S(1)}, f32[128,896]{1,0:T(8,128)S(1)}, bf16[128,896]{1,0:T(8,128)(2,1)S(1)}, bf16[128,896]{1,0:T(8,128)(2,...) custom-call(s32[3,88]{1,0:T(4,128)S(1)} %get-tuple-element.128.ent, ...), custom_call_target="tpu_custom_call" | custom-call | flops 1000000000 | bytes 12000000 | tf_op jit(solution)/shard_map/query_grads/pallas_call | solution.py:323
  89.9 2.7 %code_grads.3 = (f32[128,896]{1,0:T(8,128)S(1)}, bf16[128,896]{1,0:T(8,128)(2,1)S(1)}, bf16[128,896]{1,0:T(8,128)(2,1)S(1)}, bf16[128,896]{1,0:T(8,128)(2,1)S(1)}, bf16[4,128,896]{2,1,0:T(8,128)(2,1)S(1)}) custom-call(s32[3,88]{1,0:T(4,128)S(1)} %get-tuple-element.128.ent, bf16[18,128,128]{2,1,0:T(8,128)(2,1)S(1)} %get-tuple-element.152.g_ref, ...), custom_call_target="tpu_custom_call" | custom-call | flops 1000000000 | bytes 12000000 | tf_op jit(solution)/shard_map/reduce/code_grads/pallas_call | solution.py:368
  94.3 2.5 %collective-permute-start.72 = (bf16[64,896]{1,0:T(8,128)(2,1)S(1)}, bf16[64,896]{1,0:T(8,128)(2,1)S(1)}, u32[]{:S(2)}, u32[]{:S(2)}) collective-permute-start(bf16[64,896]{1,0:T(8,128)(2,1)S(1)} %get-tuple-element.143), channel_id=1, source_target_pairs={{0,56},{8,0},{16,8},{24,16},{32,24},{40,32},{48,40},{56,48},{1,57}... | collective-permute-start | bytes 344072 | tf_op jit(solution)/shard_map/reduce/ppermute | solution.py:386
  96.8 3.6 %collective-permute-done.71.refs_0_ = bf16[64,896]{1,0:T(8,128)(2,1)S(1)} collective-permute-done((bf16[64,896]{1,0:T(8,128)(2,1)S(1)}, bf16[64,896]{1,0:T(8,128)(2,1)S(1)}, u32[]{:S(2)}, u32[]{:S(2)}) %collective-permute-start.71) | collective-permute-done | bytes 114720 | tf_op jit(solution)/shard_map/reduce/ppermute | solution.py:386
  104.7 5.1 %collective-permute-done.73.refs_0_ = bf16[128,896]{1,0:T(8,128)(2,1)S(1)} collective-permute-done((bf16[128,896]{1,0:T(8,128)(2,1)S(1)}, bf16[128,896]{1,0:T(8,128)(2,1)S(1)}, u32[]{:S(2)}, u32[]{:S(2)}) %collective-permute-start.73) | collective-permute-done | bytes 229408 | tf_op jit(solution)/shard_map/reduce/ppermute | solution.py:386
  110.0 2.3 %collective-permute-start.75 = (bf16[128,896]{1,0:T(8,128)(2,1)S(1)}, bf16[128,896]{1,0:T(8,128)(2,1)S(1)}, u32[]{:S(2)}, u32[]{:S(2)}) collective-permute-start(bf16[128,896]{1,0:T(8,128)(2,1)S(1)} %get-tuple-element.150), channel_id=1, source_target_pairs={{0,8},{8,16},{16,24},{24,32},{32,40},{40,48},{48,56},{56,0},{1,9},... | collective-permute-start | bytes 688136 | tf_op jit(solution)/shard_map/reduce/ppermute | solution.py:386
  113.5 3.0 %collective-permute-start.78 = (bf16[128,896]{1,0:T(8,128)(2,1)S(1)}, bf16[128,896]{1,0:T(8,128)(2,1)S(1)}, u32[]{:S(2)}, u32[]{:S(2)}) collective-permute-start(bf16[128,896]{1,0:T(8,128)(2,1)S(1)} %get-tuple-element.157), channel_id=1, source_target_pairs={{0,64},{64,128},{128,192},{192,0},{1,65},{65,129},{129,193},{193,1... | collective-permute-start | bytes 688136 | tf_op jit(solution)/shard_map/reduce/ppermute | solution.py:386
  118.3 6.2 %collective-permute-done.78 = bf16[128,896]{1,0:T(8,128)(2,1)S(1)} collective-permute-done((bf16[128,896]{1,0:T(8,128)(2,1)S(1)}, bf16[128,896]{1,0:T(8,128)(2,1)S(1)}, u32[]{:S(2)}, u32[]{:S(2)}) %collective-permute-start.78) | collective-permute-done | bytes 229408 | tf_op jit(solution)/shard_map/reduce/ppermute | solution.py:386
  125.9 2.1 %collective-permute-done.80 = bf16[128,896]{1,0:T(8,128)(2,1)S(1)} collective-permute-done((bf16[128,896]{1,0:T(8,128)(2,1)S(1)}, bf16[128,896]{1,0:T(8,128)(2,1)S(1)}, u32[]{:S(2)}, u32[]{:S(2)}) %collective-permute-start.80) | collective-permute-done | bytes 229408 | tf_op jit(solution)/shard_map/reduce/ppermute | solution.py:386
  128.1 3.2 %collective-permute-start.82 = (bf16[128,896]{1,0:T(8,128)(2,1)S(1)}, bf16[128,896]{1,0:T(8,128)(2,1)S(1)}, u32[]{:S(2)}, u32[]{:S(2)}) collective-permute-start(bf16[128,896]{1,0:T(8,128)(2,1)S(1)} %get-tuple-element.165), channel_id=1, source_target_pairs={{0,56},{8,0},{16,8},{24,16},{32,24},{40,32},{48,40},{56,48},{1,57}... | collective-permute-start | bytes 688136 | tf_op jit(solution)/shard_map/reduce/ppermute | solution.py:386
  132.3 4.0 %collective-permute-done.81 = bf16[128,896]{1,0:T(8,128)(2,1)S(1)} collective-permute-done((bf16[128,896]{1,0:T(8,128)(2,1)S(1)}, bf16[128,896]{1,0:T(8,128)(2,1)S(1)}, u32[]{:S(2)}, u32[]{:S(2)}) %collective-permute-start.81) | collective-permute-done | bytes 229408 | tf_op jit(solution)/shard_map/reduce/ppermute | solution.py:386
  (70 shorter events, 32.6 us)
Async XLA Ops:
  0.6 11.7 %collective-permute-start.44 = (bf16[128,896]{1,0:T(8,128)(2,1)}, bf16[128,896]{1,0:T(8,128)(2,1)S(1)}, u32[]{:S(2)}, u32[]{:S(2)}) collective-permute-start(bf16[128,896]{1,0:T(8,128)(2,1)} %refs_0_.3), channel_id=1, source_target_pairs={{0,8},{8,16},{16,24},{24,32},{32,40},{40,48},{48,56},{56,0},{1,9},... | collective-permute-start | bytes 688136 | tf_op jit(solution)/shard_map/gather/ppermute | solution.py:386
  2.6 9.8 %collective-permute-start.45 = (bf16[128,896]{1,0:T(8,128)(2,1)}, bf16[128,896]{1,0:T(8,128)(2,1)S(1)}, u32[]{:S(2)}, u32[]{:S(2)}) collective-permute-start(bf16[128,896]{1,0:T(8,128)(2,1)} %refs_0_.3), channel_id=1, source_target_pairs={{0,56},{8,0},{16,8},{24,16},{32,24},{40,32},{48,40},{56,48},{1,57}... | collective-permute-start | bytes 688136 | tf_op jit(solution)/shard_map/gather/ppermute | solution.py:386
  12.4 8.0 %collective-permute-start.48 = (bf16[128,896]{1,0:T(8,128)(2,1)S(1)}, bf16[128,896]{1,0:T(8,128)(2,1)S(1)}, u32[]{:S(2)}, u32[]{:S(2)}) collective-permute-start(bf16[128,896]{1,0:T(8,128)(2,1)S(1)} %collective-permute-done.44.refs_4_), channel_id=1, source_target_pairs={{0,8},{8,16},{16,24},{24,32},{32,40},{40,48},{48,56},{56,0},{1,9},... | collective-permute-start | bytes 688136 | tf_op jit(solution)/shard_map/gather/ppermute | solution.py:386
  12.4 8.0 %collective-permute-start.46 = (bf16[128,896]{1,0:T(8,128)(2,1)S(1)}, bf16[128,896]{1,0:T(8,128)(2,1)S(1)}, u32[]{:S(2)}, u32[]{:S(2)}) collective-permute-start(bf16[128,896]{1,0:T(8,128)(2,1)S(1)} %collective-permute-done.45.refs_1_), channel_id=1, source_target_pairs={{0,56},{8,0},{16,8},{24,16},{32,24},{40,32},{48,40},{56,48},{1,57}... | collective-permute-start | bytes 688136 | tf_op jit(solution)/shard_map/gather/ppermute | solution.py:386
  15.6 12.6 %collective-permute-start.53 = (bf16[128,896]{1,0:T(8,128)(2,1)}, bf16[128,896]{1,0:T(8,128)(2,1)S(1)}, u32[]{:S(2)}, u32[]{:S(2)}) collective-permute-start(bf16[128,896]{1,0:T(8,128)(2,1)} %refs_4_.1), channel_id=1, source_target_pairs={{0,192},{64,0},{128,64},{192,128},{1,193},{65,1},{129,65},{193,129... | collective-permute-start | bytes 688136 | tf_op jit(solution)/shard_map/gather/ppermute | solution.py:386
  16.4 11.8 %collective-permute-start.55 = (bf16[128,896]{1,0:T(8,128)(2,1)}, bf16[128,896]{1,0:T(8,128)(2,1)S(1)}, u32[]{:S(2)}, u32[]{:S(2)}) collective-permute-start(bf16[128,896]{1,0:T(8,128)(2,1)} %refs_4_.1), channel_id=1, source_target_pairs={{0,128},{64,192},{128,0},{192,64},{1,129},{65,193},{129,1},{193,65... | collective-permute-start | bytes 688136 | tf_op jit(solution)/shard_map/gather/ppermute | solution.py:386
  17.3 11.5 %collective-permute-start.57 = (bf16[128,896]{1,0:T(8,128)(2,1)}, bf16[128,896]{1,0:T(8,128)(2,1)S(1)}, u32[]{:S(2)}, u32[]{:S(2)}) collective-permute-start(bf16[128,896]{1,0:T(8,128)(2,1)} %refs_4_.1), channel_id=1, source_target_pairs={{0,64},{64,128},{128,192},{192,0},{1,65},{65,129},{129,193},{193,1... | collective-permute-start | bytes 688136 | tf_op jit(solution)/shard_map/gather/ppermute | solution.py:386
  20.4 8.4 %collective-permute-start.49 = (bf16[128,896]{1,0:T(8,128)(2,1)S(1)}, bf16[128,896]{1,0:T(8,128)(2,1)S(1)}, u32[]{:S(2)}, u32[]{:S(2)}) collective-permute-start(bf16[128,896]{1,0:T(8,128)(2,1)S(1)} %collective-permute-done.48.refs_5_), channel_id=1, source_target_pairs={{0,8},{8,16},{16,24},{24,32},{32,40},{40,48},{48,56},{56,0},{1,9},... | collective-permute-start | bytes 688136 | tf_op jit(solution)/shard_map/gather/ppermute | solution.py:386
  20.4 8.9 %collective-permute-start.47 = (bf16[128,896]{1,0:T(8,128)(2,1)S(1)}, bf16[128,896]{1,0:T(8,128)(2,1)S(1)}, u32[]{:S(2)}, u32[]{:S(2)}) collective-permute-start(bf16[128,896]{1,0:T(8,128)(2,1)S(1)} %collective-permute-done.46.refs_2_), channel_id=1, source_target_pairs={{0,56},{8,0},{16,8},{24,16},{32,24},{40,32},{48,40},{56,48},{1,57}... | collective-permute-start | bytes 688136 | tf_op jit(solution)/shard_map/gather/ppermute | solution.py:386
  29.4 6.4 %collective-permute-start.50 = (bf16[64,896]{1,0:T(8,128)(2,1)S(1)}, bf16[64,896]{1,0:T(8,128)(2,1)S(1)}, u32[]{:S(2)}, u32[]{:S(2)}) collective-permute-start(bf16[64,896]{1,0:T(8,128)(2,1)S(1)} %slice.24), channel_id=1, source_target_pairs={{0,8},{8,16},{16,24},{24,32},{32,40},{40,48},{48,56},{56,0},{1,9},... | collective-permute-start | bytes 344072 | tf_op jit(solution)/shard_map/gather/ppermute | solution.py:386
  30.1 5.6 %collective-permute-start.51 = (bf16[64,896]{1,0:T(8,128)(2,1)S(1)}, bf16[64,896]{1,0:T(8,128)(2,1)S(1)}, u32[]{:S(2)}, u32[]{:S(2)}) collective-permute-start(bf16[64,896]{1,0:T(8,128)(2,1)S(1)} %slice.25), channel_id=1, source_target_pairs={{0,56},{8,0},{16,8},{24,16},{32,24},{40,32},{48,40},{56,48},{1,57}... | collective-permute-start | bytes 344072 | tf_op jit(solution)/shard_map/gather/ppermute | solution.py:386
  38.3 10.3 %collective-permute-start.59 = (f32[18,32,128]{2,1,0:T(8,128)S(1)}, f32[18,32,128]{2,1,0:T(8,128)S(1)}, u32[]{:S(2)}, u32[]{:S(2)}) collective-permute-start(f32[18,32,128]{2,1,0:T(8,128)S(1)} %get-tuple-element.132), channel_id=1, source_target_pairs={{0,1},{1,2},{2,3},{3,0},{4,5},{5,6},{6,7},{7,4},{8,9},{9,10},{10,1... | collective-permute-start | bytes 884744 | tf_op jit(solution)/shard_map/scores_over_x/ppermute | solution.py:386
  39.9 14.9 %collective-permute-start.60 = (f32[18,32,128]{2,1,0:T(8,128)S(1)}, f32[18,32,128]{2,1,0:T(8,128)S(1)}, u32[]{:S(2)}, u32[]{:S(2)}) collective-permute-start(f32[18,32,128]{2,1,0:T(8,128)S(1)} %get-tuple-element.133), channel_id=1, source_target_pairs={{0,2},{1,3},{2,0},{3,1},{4,6},{5,7},{6,4},{7,5},{8,10},{9,11},{10,... | collective-permute-start | bytes 884744 | tf_op jit(solution)/shard_map/scores_over_x/ppermute | solution.py:386
  42.6 12.2 %collective-permute-start.61 = (f32[18,32,128]{2,1,0:T(8,128)S(1)}, f32[18,32,128]{2,1,0:T(8,128)S(1)}, u32[]{:S(2)}, u32[]{:S(2)}) collective-permute-start(f32[18,32,128]{2,1,0:T(8,128)S(1)} %get-tuple-element.134), channel_id=1, source_target_pairs={{0,3},{1,0},{2,1},{3,2},{4,7},{5,4},{6,5},{7,6},{8,11},{9,8},{10,9... | collective-permute-start | bytes 884744 | tf_op jit(solution)/shard_map/scores_over_x/ppermute | solution.py:386
  59.8 4.9 %collective-permute-start.64 = (f32[2,32,128]{2,1,0:T(8,128)S(1)}, f32[2,32,128]{2,1,0:T(8,128)S(1)}, u32[]{:S(2)}, u32[]{:S(2)}) collective-permute-start(f32[2,32,128]{2,1,0:T(8,128)S(1)} %get-tuple-element.137.refs_0_), channel_id=1, source_target_pairs={{0,16},{8,24},{16,0},{24,8},{32,48},{40,56},{48,32},{56,40},{1,17}... | collective-permute-start | bytes 98312 | tf_op jit(solution)/shard_map/stats/ppermute | solution.py:416
  66.8 7.9 %collective-permute-start.66 = (f32[2,32,128]{2,1,0:T(8,128)S(1)}, f32[2,32,128]{2,1,0:T(8,128)S(1)}, u32[]{:S(2)}, u32[]{:S(2)}) collective-permute-start(f32[2,32,128]{2,1,0:T(8,128)S(1)} %get-tuple-element.139.za), channel_id=1, source_target_pairs={{0,32},{8,40},{16,48},{24,56},{32,0},{40,8},{48,16},{56,24},{1,33}... | collective-permute-start | bytes 98312 | tf_op jit(solution)/shard_map/stats/ppermute | solution.py:416
  70.0 5.4 %collective-permute-start.67 = (f32[2,32,128]{2,1,0:T(8,128)S(1)}, f32[2,32,128]{2,1,0:T(8,128)S(1)}, u32[]{:S(2)}, u32[]{:S(2)}) collective-permute-start(f32[2,32,128]{2,1,0:T(8,128)S(1)} %get-tuple-element.140.ya), channel_id=1, source_target_pairs={{0,128},{64,192},{128,0},{192,64},{1,129},{65,193},{129,1},{193,65... | collective-permute-start | bytes 98312 | tf_op jit(solution)/shard_map/stats/ppermute | solution.py:416
  76.4 6.8 %collective-permute-start.68 = (bf16[18,32,128]{2,1,0:T(8,128)(2,1)S(1)}, bf16[18,32,128]{2,1,0:T(8,128)(2,1)S(1)}, u32[]{:S(2)}, u32[]{:S(2)}) collective-permute-start(bf16[18,32,128]{2,1,0:T(8,128)(2,1)S(1)} %coefficients.1.refs_0_), channel_id=1, source_target_pairs={{0,3},{1,0},{2,1},{3,2},{4,7},{5,4},{6,5},{7,6},{8,11},{9,8},{10,9... | collective-permute-start | bytes 442376 | tf_op jit(solution)/shard_map/coefs_over_x/ppermute | solution.py:386
  78.9 6.7 %collective-permute-start.69 = (bf16[18,32,128]{2,1,0:T(8,128)(2,1)S(1)}, bf16[18,32,128]{2,1,0:T(8,128)(2,1)S(1)}, u32[]{:S(2)}, u32[]{:S(2)}) collective-permute-start(bf16[18,32,128]{2,1,0:T(8,128)(2,1)S(1)} %coefficients.1.refs_0_), channel_id=1, source_target_pairs={{0,2},{1,3},{2,0},{3,1},{4,6},{5,7},{6,4},{7,5},{8,10},{9,11},{10,... | collective-permute-start | bytes 442376 | tf_op jit(solution)/shard_map/coefs_over_x/ppermute | solution.py:386
  80.0 7.1 %collective-permute-start.70 = (bf16[18,32,128]{2,1,0:T(8,128)(2,1)S(1)}, bf16[18,32,128]{2,1,0:T(8,128)(2,1)S(1)}, u32[]{:S(2)}, u32[]{:S(2)}) collective-permute-start(bf16[18,32,128]{2,1,0:T(8,128)(2,1)S(1)} %coefficients.1.refs_0_), channel_id=1, source_target_pairs={{0,1},{1,2},{2,3},{3,0},{4,5},{5,6},{6,7},{7,4},{8,9},{9,10},{10,1... | collective-permute-start | bytes 442376 | tf_op jit(solution)/shard_map/coefs_over_x/ppermute | solution.py:386
  92.6 20.7 %collective-permute-start.77 = (bf16[4,128,896]{2,1,0:T(8,128)(2,1)S(1)}, bf16[4,128,896]{2,1,0:T(8,128)(2,1)S(1)}, u32[]{:S(2)}, u32[]{:S(2)}) collective-permute-start(bf16[4,128,896]{2,1,0:T(8,128)(2,1)S(1)} %get-tuple-element.153), channel_id=1, source_target_pairs={{0,4},{4,0},{1,5},{5,1},{2,6},{6,2},{3,7},{7,3},{8,12},{12,8},{9,1... | collective-permute-start | bytes 2752520 | tf_op jit(solution)/shard_map/reduce/ppermute | solution.py:386
  92.7 7.8 %collective-permute-start.71 = (bf16[64,896]{1,0:T(8,128)(2,1)S(1)}, bf16[64,896]{1,0:T(8,128)(2,1)S(1)}, u32[]{:S(2)}, u32[]{:S(2)}) collective-permute-start(bf16[64,896]{1,0:T(8,128)(2,1)S(1)} %get-tuple-element.142), channel_id=1, source_target_pairs={{0,8},{8,16},{16,24},{24,32},{32,40},{40,48},{48,56},{56,0},{1,9},... | collective-permute-start | bytes 344072 | tf_op jit(solution)/shard_map/reduce/ppermute | solution.py:386
  94.3 7.0 %collective-permute-start.72 = (bf16[64,896]{1,0:T(8,128)(2,1)S(1)}, bf16[64,896]{1,0:T(8,128)(2,1)S(1)}, u32[]{:S(2)}, u32[]{:S(2)}) collective-permute-start(bf16[64,896]{1,0:T(8,128)(2,1)S(1)} %get-tuple-element.143), channel_id=1, source_target_pairs={{0,56},{8,0},{16,8},{24,16},{32,24},{40,32},{48,40},{56,48},{1,57}... | collective-permute-start | bytes 344072 | tf_op jit(solution)/shard_map/reduce/ppermute | solution.py:386
  101.4 8.4 %collective-permute-start.73 = (bf16[128,896]{1,0:T(8,128)(2,1)S(1)}, bf16[128,896]{1,0:T(8,128)(2,1)S(1)}, u32[]{:S(2)}, u32[]{:S(2)}) collective-permute-start(bf16[128,896]{1,0:T(8,128)(2,1)S(1)} %get-tuple-element.146), channel_id=1, source_target_pairs={{0,8},{8,16},{16,24},{24,32},{32,40},{40,48},{48,56},{56,0},{1,9},... | collective-permute-start | bytes 688136 | tf_op jit(solution)/shard_map/reduce/ppermute | solution.py:386
  103.2 6.6 %collective-permute-start.74 = (bf16[128,896]{1,0:T(8,128)(2,1)S(1)}, bf16[128,896]{1,0:T(8,128)(2,1)S(1)}, u32[]{:S(2)}, u32[]{:S(2)}) collective-permute-start(bf16[128,896]{1,0:T(8,128)(2,1)S(1)} %get-tuple-element.147), channel_id=1, source_target_pairs={{0,56},{8,0},{16,8},{24,16},{32,24},{40,32},{48,40},{56,48},{1,57}... | collective-permute-start | bytes 688136 | tf_op jit(solution)/shard_map/reduce/ppermute | solution.py:386
  110.0 7.5 %collective-permute-start.75 = (bf16[128,896]{1,0:T(8,128)(2,1)S(1)}, bf16[128,896]{1,0:T(8,128)(2,1)S(1)}, u32[]{:S(2)}, u32[]{:S(2)}) collective-permute-start(bf16[128,896]{1,0:T(8,128)(2,1)S(1)} %get-tuple-element.150), channel_id=1, source_target_pairs={{0,8},{8,16},{16,24},{24,32},{32,40},{40,48},{48,56},{56,0},{1,9},... | collective-permute-start | bytes 688136 | tf_op jit(solution)/shard_map/reduce/ppermute | solution.py:386
  112.3 6.0 %collective-permute-start.76 = (bf16[128,896]{1,0:T(8,128)(2,1)S(1)}, bf16[128,896]{1,0:T(8,128)(2,1)S(1)}, u32[]{:S(2)}, u32[]{:S(2)}) collective-permute-start(bf16[128,896]{1,0:T(8,128)(2,1)S(1)} %get-tuple-element.151), channel_id=1, source_target_pairs={{0,56},{8,0},{16,8},{24,16},{32,24},{40,32},{48,40},{56,48},{1,57}... | collective-permute-start | bytes 688136 | tf_op jit(solution)/shard_map/reduce/ppermute | solution.py:386
  113.5 11.1 %collective-permute-start.78 = (bf16[128,896]{1,0:T(8,128)(2,1)S(1)}, bf16[128,896]{1,0:T(8,128)(2,1)S(1)}, u32[]{:S(2)}, u32[]{:S(2)}) collective-permute-start(bf16[128,896]{1,0:T(8,128)(2,1)S(1)} %get-tuple-element.157), channel_id=1, source_target_pairs={{0,64},{64,128},{128,192},{192,0},{1,65},{65,129},{129,193},{193,1... | collective-permute-start | bytes 688136 | tf_op jit(solution)/shard_map/reduce/ppermute | solution.py:386
  116.4 9.4 %collective-permute-start.79 = (bf16[128,896]{1,0:T(8,128)(2,1)S(1)}, bf16[128,896]{1,0:T(8,128)(2,1)S(1)}, u32[]{:S(2)}, u32[]{:S(2)}) collective-permute-start(bf16[128,896]{1,0:T(8,128)(2,1)S(1)} %get-tuple-element.158), channel_id=1, source_target_pairs={{0,128},{64,192},{128,0},{192,64},{1,129},{65,193},{129,1},{193,65... | collective-permute-start | bytes 688136 | tf_op jit(solution)/shard_map/reduce/ppermute | solution.py:386
  116.5 11.5 %collective-permute-start.80 = (bf16[128,896]{1,0:T(8,128)(2,1)S(1)}, bf16[128,896]{1,0:T(8,128)(2,1)S(1)}, u32[]{:S(2)}, u32[]{:S(2)}) collective-permute-start(bf16[128,896]{1,0:T(8,128)(2,1)S(1)} %get-tuple-element.159), channel_id=1, source_target_pairs={{0,192},{64,0},{128,64},{192,128},{1,193},{65,1},{129,65},{193,129... | collective-permute-start | bytes 688136 | tf_op jit(solution)/shard_map/reduce/ppermute | solution.py:386
  128.0 8.2 %collective-permute-start.81 = (bf16[128,896]{1,0:T(8,128)(2,1)S(1)}, bf16[128,896]{1,0:T(8,128)(2,1)S(1)}, u32[]{:S(2)}, u32[]{:S(2)}) collective-permute-start(bf16[128,896]{1,0:T(8,128)(2,1)S(1)} %get-tuple-element.164), channel_id=1, source_target_pairs={{0,8},{8,16},{16,24},{24,32},{32,40},{40,48},{48,56},{56,0},{1,9},... | collective-permute-start | bytes 688136 | tf_op jit(solution)/shard_map/reduce/ppermute | solution.py:386
  128.1 8.1 %collective-permute-start.82 = (bf16[128,896]{1,0:T(8,128)(2,1)S(1)}, bf16[128,896]{1,0:T(8,128)(2,1)S(1)}, u32[]{:S(2)}, u32[]{:S(2)}) collective-permute-start(bf16[128,896]{1,0:T(8,128)(2,1)S(1)} %get-tuple-element.165), channel_id=1, source_target_pairs={{0,56},{8,0},{16,8},{24,16},{32,24},{40,32},{48,40},{56,48},{1,57}... | collective-permute-start | bytes 688136 | tf_op jit(solution)/shard_map/reduce/ppermute | solution.py:386
  (10 other events, 74.1 us)
